TPU v7x, 32 devices: a whole 2x2x4 slice. The times are simulated.
32 devices in a mesh: segment: 4 (over z), band: 8 (over y, x, core).
Axes of the slice: x: 2, y: 2, z: 4, core: 2. Of those that a mesh axis runs over, the one named last changes fastest.
Arguments:
- clip: bfloat16 [2, 32, 160, 128], P(None, 'band'), may hold values from -6 to 6
- caches: bfloat16 [4, 4, 2, 32, 160, 128], P('segment', None, None, 'band'), may hold values from -4 to 4
- weights: bfloat16 [4, 4, 9, 3, 128, 128], P('segment'), may hold values from -0.109375 to 0.109375
- biases: float32 [4, 4, 128], P('segment'), may hold values from -2 to 2
- section_layers: int32 [4], P('segment'), may hold values from 1 to 4, as said below
Outputs:
- section_out: bfloat16 [4, 2, 32, 160, 128], P('segment', None, 'band')
Inputs may be any that keep to these rules, and one draw needn't show every extreme that they name: `section_layers`: each section has 1 to 4 layers, and some section has exactly 4.
All inputs are finite; a program needn't handle non-finite values.
Results may differ from a plain program's by a relative error of at most 0.024.
Values may be sent and summed in bfloat16 or wider, within the bound.
No kernel may reach another device: no remote copies, remote signals or barrier semaphores. Data moves between devices by JAX's collectives and lax.ppermute only.
A program may use at most 128 MiB of HBM per device.

v0:
```python
import functools

import jax
import jax.numpy as jnp
from jax import lax
from jax.experimental import pallas as pl
from jax.experimental.pallas import tpu as pltpu
from jax.sharding import PartitionSpec as P

LIMIT = 28 * 1024 * 1024
HISTORY_LIMIT = 52 * 1024 * 1024
F32 = jnp.float32
PAD = 8
BF16 = jnp.bfloat16


def message_starts(layers):
    starts = [0]
    for level in range(layers):
        starts.append(starts[-1] + layers - level)
    return starts


def taps_into(s_ref, row, a, line):
    width, channels = a.shape
    line[PAD : PAD + width] = a
    s_ref[row, :, 0:channels] = line[PAD - 1 : PAD - 1 + width].astype(BF16)
    s_ref[row, :, channels : 2 * channels] = a.astype(BF16)
    s_ref[row, :, 2 * channels : 3 * channels] = line[PAD + 1 : PAD + 1 + width].astype(BF16)


def clear_lines(lines):
    edge = jnp.zeros((PAD, lines.shape[2]), F32)
    for i in range(lines.shape[0]):
        lines[i, 0:PAD] = edge
        lines[i, lines.shape[1] - PAD :] = edge


def rows_dot(s_ref, first, count, w, layer, times):
    width, depth = s_ref.shape[1:]
    taps = jnp.concatenate([s_ref[pl.ds(first + i, count)].reshape(count * width, depth) for i in range(3)], axis=1)
    weights = jnp.concatenate([jnp.concatenate([w[layer, k, t] for t in times], axis=1) for k in range(9)], axis=0)
    return jnp.dot(taps, weights, preferred_element_type=F32)


def pairs_dot(first, count, w, layer, *terms):
    width, depth = terms[0][0].shape[1:]
    channels = depth // 3
    taps = jnp.concatenate(
        [
            jnp.concatenate([s_ref[first + i + 2 * p] for p in range(count)], axis=0)
            for s_ref, _ in terms
            for i in range(4)
        ],
        axis=1,
    )
    zero = jnp.zeros((channels, channels), BF16)

    def tap(i, j, time):
        return w[layer, 3 * i + j, time] if 0 <= i < 3 else zero

    weights = jnp.concatenate(
        [
            jnp.concatenate([tap(i, j, time), tap(i - 1, j, time)], axis=1)
            for _, time in terms
            for i in range(4)
            for j in range(3)
        ],
        axis=0,
    )
    total = jnp.dot(taps, weights, preferred_element_type=F32)
    upper = total[:, :channels].reshape(count, 1, width, channels)
    lower = total[:, channels:].reshape(count, 1, width, channels)
    return jnp.concatenate([upper, lower], axis=1).reshape(2 * count, width, channels)


def history_kernel(frame, flags, caches, w, sums, inner, cross, *refs):
    layers, _, rows, width, channels = caches.shape
    begin = layers - flags[2]
    if frame == 0:
        done, held, wb, s, lines, sems = refs
    else:
        held, wb = caches, w
        s, lines = refs

    def loads(layer):
        return [
            pltpu.make_async_copy(caches.at[layer], held.at[layer], sems.at[layer, 0]),
            pltpu.make_async_copy(w.at[layer, :, 0:2], wb.at[layer], sems.at[layer, 1]),
        ]

    if frame == 0:
        for layer in range(layers):

            @pl.when(layer < flags[2])
            def _(layer=layer):
                for copy in loads(layer):
                    copy.start()

    clear_lines(lines)
    for f in range(frame, 2):
        s[f, 0:2] = jnp.zeros((2,) + s.shape[2:], BF16)
        s[f, rows + 2 : rows + 4] = jnp.zeros((2,) + s.shape[2:], BF16)

    def layer_step(layer, _):
        if frame == 0:
            history, taps = loads(layer)
            history.wait()

        def build(row, _):
            for f in range(frame, 2):
                taps_into(s.at[f], row + 2, held[layer, f, row].astype(F32), lines.at[f])
            return 0

        lax.fori_loop(0, rows, build, 0)
        if frame == 0:
            taps.wait()
        terms = [(s.at[f], f - frame) for f in range(frame, 2)]
        sums[begin + layer] = pairs_dot(0, (rows + 2) // 2, wb, layer, *terms).astype(BF16)
        return 0

    lax.fori_loop(0, flags[2], layer_step, 0)
    starts = message_starts(layers)

    def messages(up, down):
        for level in range(layers):
            reach = layers - level
            up[starts[level] : starts[level + 1]] = sums[level, 0:reach]
            down[starts[level] : starts[level + 1]] = sums[level, rows + 2 - reach : rows + 2]

    @pl.when(flags[1] % 2 == 0)
    def _():
        messages(cross, inner)

    @pl.when(flags[1] % 2 != 0)
    def _():
        messages(inner, cross)


def pieces(count):
    parts, at = [], 0
    while at < count:
        step = 4 if count - at in (4, 8) else min(6, count - at)
        parts.append((at, step))
        at += step
    return parts


def tick_kernel(tick, segments, bands, flags, w, bias, *refs):
    zero, one = tick < segments, tick > 0
    refs = list(refs)

    def take(count):
        found, refs[:count] = refs[:count], []
        return found

    clip = take(3) if tick < 2 else None
    own, inner, cross = take(3) if one else (None, None, None)
    sums0 = take(3) if zero else None
    sums1 = take(3) if one else None
    behind = take(1)[0] if one else None
    done = take(1)
    x_out = take(1)[0]
    ahead = take(1)[0] if zero else None
    done_out, x, s, lines, part, sem = refs
    rows, width, channels = x_out.shape
    layers = w.shape[0]
    starts = message_starts(layers)
    band = flags[1]
    begin = layers - flags[2]
    low = jnp.where(band == 0, rows, 0)
    high = jnp.where(band == bands - 1, 2 * rows, 3 * rows)

    def run(frame, fresh, own, inner, cross, sums, messages):
        def of(source):
            return source[frame] if fresh else source[...]

        x[rows : 2 * rows] = of(own)

        def gather(above, below, side_above, side_below):
            x[0:rows] = of(above)
            x[2 * rows : 3 * rows] = of(below)
            for level in range(layers):

                @pl.when(level >= begin)
                def _(level=level):
                    reach = layers - level
                    start, sums_above, sums_below = starts[level], messages[side_above], messages[side_below]
                    part[level, rows + 1 - reach : rows + 1] = sums_above[start : start + reach]
                    part[level, 2 * rows - 1 : 2 * rows - 1 + reach] = sums_below[start : start + reach]
                    part[level, rows + 1 : 2 * rows - 1] = sums[level, 2:rows]
                    part[level, rows] += sums[level, 1]
                    part[level, 2 * rows - 1] += sums[level, rows]
                    if reach > 1:
                        part[level, rows - 1] += sums[level, 0]
                        part[level, 2 * rows] += sums[level, rows + 1]

        @pl.when(band % 2 == 0)
        def _():
            gather(cross, inner, 1, 0)

        @pl.when(band % 2 != 0)
        def _():
            gather(inner, cross, 0, 1)

        clear_lines(lines)

        def build(row, line):
            half = x[row].astype(F32) * 0.5
            inside = jnp.logical_and(row >= low, row < high).astype(F32)
            taps_into(s, row, (half + half * jnp.tanh(half)) * inside, line)

        for level in range(layers):

            @pl.when(level >= begin)
            def _(level=level):
                layer = level - begin
                first = rows - layers + 1 + level
                count = rows + 2 * (layers - 1 - level)

                def two(i, _):
                    build(first - 1 + 2 * i, lines.at[0])
                    build(first + 2 * i, lines.at[1])
                    return 0

                lax.fori_loop(0, count // 2 + 1, two, 0)
                offset = bias[pl.ds(layer, 1), :].reshape(1, 1, channels)
                for start, step in [(0, count)] if frame == 0 else pieces(count):
                    at = first + start
                    known = part[level, at : at + step].astype(F32) + offset
                    if frame == 0:
                        total = rows_dot(s, at - 1, step, w, layer, (2, 1))
                        mine = total[:, :channels].reshape(step, width, channels)
                        ahead[level, at : at + step] = total[:, channels:].reshape(step, width, channels).astype(BF16)
                    else:
                        mine = pairs_dot(at - 1, step // 2, w, layer, (s, 2))
                        known = known + behind[level, at : at + step].astype(F32)
                    x[at : at + step] = (x[at : at + step].astype(F32) + (mine + known)).astype(BF16)

        copy = pltpu.make_async_copy(x.at[rows : 2 * rows], done_out.at[frame], sem)
        copy.start()
        x_out[...] = x[rows : 2 * rows]
        copy.wait()

    for frame, present, parts in ((0, zero, sums0), (1, one, sums1)):
        if present:
            fresh = tick == frame

            @pl.when(flags[0] == tick - frame)
            def _(frame=frame, fresh=fresh, parts=parts):
                run(frame, fresh, *(clip if fresh else (own, inner, cross)), parts[0], parts[1:])


def in_vmem(count):
    return [pl.BlockSpec(memory_space=pltpu.VMEM)] * count


def anywhere():
    return pl.BlockSpec(memory_space=pl.ANY)


def in_smem():
    return pl.BlockSpec(memory_space=pltpu.SMEM)


def history_call(frame, flags, caches, weights):
    layers, _, rows, width, channels = caches.shape
    row = (width, channels)
    message = jax.ShapeDtypeStruct((message_starts(layers)[-1],) + row, BF16)
    outs = [jax.ShapeDtypeStruct((layers, rows + 2) + row, BF16), message, message]
    specs = in_vmem(3)
    scratch = [pltpu.VMEM((2, rows + 4, width, 3 * channels), BF16), pltpu.VMEM((2, width + 2 * PAD, channels), F32)]
    if frame == 0:
        outs.append(jax.ShapeDtypeStruct((2, rows) + row, BF16))
        specs.append(anywhere())
        scratch = [
            pltpu.VMEM(caches.shape, BF16),
            pltpu.VMEM((layers, 9, 2, channels, channels), BF16),
            *scratch,
            pltpu.SemaphoreType.DMA((layers, 2)),
        ]
    pixels = layers * (rows + 2) * width
    return pl.pallas_call(
        functools.partial(history_kernel, frame),
        out_shape=tuple(outs),
        in_specs=[in_smem()] + ([anywhere()] * 2 if frame == 0 else in_vmem(2)),
        out_specs=tuple(specs),
        scratch_shapes=scratch,
        compiler_params=pltpu.CompilerParams(vmem_limit_bytes=HISTORY_LIMIT if frame == 0 else LIMIT),
        cost_estimate=pl.CostEstimate(
            flops=pixels * 9 * 2 * (2 - frame) * channels * channels, bytes_accessed=4000000, transcendentals=0
        ),
        name="history",
    )(flags, caches, weights)


def tick_call(tick, segments, bands, flags, clip, received, weights, biases, sums0, sums1, behind, done):
    layers, _, _, channels, _ = weights.shape
    rows, width = done.shape[1:3]
    every = (layers, 3 * rows, width, channels)
    pixels = sum(rows + 2 * level for level in range(layers)) * width
    zero, one = tick < segments, tick > 0
    extra = (list(clip) if tick < 2 else []) + (list(received) if one else [])
    extra += (list(sums0) if zero else []) + (list(sums1) + [behind] if one else [])
    outs = [jax.ShapeDtypeStruct((rows, width, channels), BF16)]
    if zero:
        outs.append(jax.ShapeDtypeStruct(every, BF16))
    specs = in_vmem(len(outs)) + [anywhere()]
    outs.append(jax.ShapeDtypeStruct(done.shape, BF16))
    return pl.pallas_call(
        functools.partial(tick_kernel, tick, segments, bands),
        out_shape=tuple(outs),
        in_specs=[in_smem()] + in_vmem(2 + len(extra)) + [anywhere()],
        out_specs=tuple(specs),
        scratch_shapes=[
            pltpu.VMEM((3 * rows, width, channels), BF16),
            pltpu.VMEM((3 * rows, width, 3 * channels), BF16),
            pltpu.VMEM((2, width + 2 * PAD, channels), F32),
            pltpu.VMEM(every, BF16),
            pltpu.SemaphoreType.DMA,
        ],
        input_output_aliases={3 + len(extra): len(outs) - 1},
        compiler_params=pltpu.CompilerParams(vmem_limit_bytes=LIMIT),
        cost_estimate=pl.CostEstimate(
            flops=pixels * 18 * 2 * channels * channels, bytes_accessed=4000000, transcendentals=pixels * channels
        ),
        name="tick",
    )(flags, weights, biases, *extra, done)


def per_device(clip, caches, weights, biases, section_layers):
    segments = lax.axis_size("segment")
    bands = lax.axis_size("band")
    caches, weights, biases = caches[0], weights[0], biases[0]
    flags = jnp.stack([lax.axis_index("segment"), lax.axis_index("band"), section_layers[0]]).astype(jnp.int32)
    axes = ("segment", "band")
    in_chip = [(b, b ^ 1) for b in range(bands)]
    between = [(b, b + 1) for b in range(1, bands - 1, 2)] + [(b + 1, b) for b in range(1, bands - 1, 2)]
    straight = [(b, b) for b in range(bands)]

    def swap(value, pairs, chosen):
        return lax.ppermute(value, axes, [(s * bands + a, s * bands + b) for s in chosen for a, b in pairs])

    def ahead(value, pairs, sources):
        return lax.ppermute(value, axes, [(s * bands + a, (s + 1) * bands + b) for s in sources for a, b in pairs])

    def lender(value, pairs):
        source = min(1, segments - 1)
        return lax.ppermute(value, axes, [(source * bands + a, b) for a, b in pairs])

    everyone = range(segments)
    clip_cross = lender(clip, between)
    clip_in = swap(clip, in_chip, [0])
    sums, inner, cross, done = history_call(0, flags, caches, weights)
    sums0 = (sums, swap(inner, in_chip, everyone), swap(cross, between, everyone))
    caches, clip_cross, _ = lax.optimization_barrier((caches, clip_cross, sums))
    sums, inner, cross = history_call(1, flags, caches, weights)
    sums1 = (sums, swap(inner, in_chip, everyone), swap(cross, between, everyone))
    halves = (clip, clip_in, clip_cross)
    received = behind = None
    for tick in range(segments + 1):
        x, *later, done = tick_call(
            tick, segments, bands, flags, halves, received, weights, biases, sums0, sums1, behind, done
        )
        if tick < segments:
            (behind,) = later
            sources = [s for s in (tick, tick - 1) if 0 <= s < segments - 1]
            own, cross = ahead(x, straight, sources), ahead(x, between, sources)
            received = (own, swap(own, in_chip, [s + 1 for s in sources]), cross)
    return done[None]


def solution(mesh):
    placed = (
        P(None, "band", None, None),
        P("segment", None, None, "band", None, None),
        P("segment", None, None, None, None, None),
        P("segment", None, None),
        P("segment"),
    )
    return jax.shard_map(
        per_device,
        mesh=mesh,
        in_specs=placed,
        out_specs=P("segment", None, "band", None, None),
        check_vma=False,
    )
```

profile of v0, /device:TPU:29, one launch (start us, length us, event | category | flops | bytes accessed | tf_op | source)
XLA Modules:
  0.0 95.3 jit_solution(5212379762510388192)
XLA Ops:
  0.0 0.7 collective-permute-start.1
  1.3 0.1 pad_add_fusion.flags
  1.4 5.3 %history.2 = (bf16[4,6,160,128]{3,2,1,0:T(8,128)(2,1)S(1)}, bf16[10,160,128]{2,1,0:T(8,128)(2,1)S(1)}, bf16[10,160,128]{2,1,0:T(8,128)(2,1)S(1)}, bf16[2,4,160,128]{3,2,1,0:T(8,128)(2,1)}) custom-call(s32[3]{0:T(128)S(1)} %pad_add_fusion.flags, bf16[4,2,4,160,128]{4,3,2,1,0:T(8,128)(2,1)} %bitcast.13, bf16[4,9,3,128,128]{4,3,2,1,0:T(8,128)(2,1)} %bitcast.6), custom_call_target="tpu_custom_call" | custom-call | flops 2264924160 | bytes 4000000 | tf_op jit(solution)/shard_map/history/pallas_call | solution.py:283
  6.8 0.7 collective-permute-start.2
  7.5 3.0 %collective-permute-start.3 = (bf16[10,160,128]{2,1,0:T(8,128)(2,1)S(1)}, bf16[10,160,128]{2,1,0:T(8,128)(2,1)S(1)}, u32[]{:S(2)}, u32[]{:S(2)}) collective-permute-start(bf16[10,160,128]{2,1,0:T(8,128)(2,1)S(1)} %get-tuple-element.30), channel_id=1, source_target_pairs={{1,2},{3,4},{5,6},{2,1},{4,3},{6,5},{9,10},{11,12},{13,14},{10,9},... | collective-permute-start | bytes 1228808 | tf_op jit(solution)/shard_map/ppermute | solution.py:342
  10.5 0.7 collective-permute-start
  11.3 2.6 %history.3 = (bf16[4,6,160,128]{3,2,1,0:T(8,128)(2,1)S(1)}, bf16[10,160,128]{2,1,0:T(8,128)(2,1)S(1)}, bf16[10,160,128]{2,1,0:T(8,128)(2,1)S(1)}) custom-call(s32[3]{0:T(128)S(1)} %pad_add_fusion.flags, bf16[4,2,4,160,128]{4,3,2,1,0:T(8,128)(2,1)S(1)} %bitcast.14, bf16[4,9,3,128,128]{4,3,2,1,0:T(8,128)(2,1)S(1)} %bitcast.7), custom_call_target="tpu_custom_call" | custom-call | flops 1132462080 | bytes 4000000 | tf_op jit(solution)/shard_map/history/pallas_call | solution.py:283
  13.9 0.5 collective-permute-start.7
  14.4 2.1 %collective-permute-start.8 = (bf16[10,160,128]{2,1,0:T(8,128)(2,1)S(1)}, bf16[10,160,128]{2,1,0:T(8,128)(2,1)S(1)}, u32[]{:S(2)}, u32[]{:S(2)}) collective-permute-start(bf16[10,160,128]{2,1,0:T(8,128)(2,1)S(1)} %get-tuple-element.36), channel_id=1, source_target_pairs={{1,2},{3,4},{5,6},{2,1},{4,3},{6,5},{9,10},{11,12},{13,14},{10,9},... | collective-permute-start | bytes 1228808 | tf_op jit(solution)/shard_map/ppermute | solution.py:342
  16.6 2.7 %collective-permute-done.3.refs_5_.refs_8_ = bf16[10,160,128]{2,1,0:T(8,128)(2,1)S(1)} collective-permute-done((bf16[10,160,128]{2,1,0:T(8,128)(2,1)S(1)}, bf16[10,160,128]{2,1,0:T(8,128)(2,1)S(1)}, u32[]{:S(2)}, u32[]{:S(2)}) %collective-permute-start.3) | collective-permute-done | bytes 409632 | tf_op jit(solution)/shard_map/ppermute | solution.py:342
  19.2 0.6 tick.5
  19.8 0.7 collective-permute-start.4
  20.5 0.7 collective-permute-start.6
  21.2 0.7 collective-permute-start.5
  21.9 6.1 %collective-permute-done.8.refs_11_.refs_8_.refs_5_ = bf16[10,160,128]{2,1,0:T(8,128)(2,1)S(1)} collective-permute-done((bf16[10,160,128]{2,1,0:T(8,128)(2,1)S(1)}, bf16[10,160,128]{2,1,0:T(8,128)(2,1)S(1)}, u32[]{:S(2)}, u32[]{:S(2)}) %collective-permute-start.8) | collective-permute-done | bytes 409632 | tf_op jit(solution)/shard_map/ppermute | solution.py:342
  28.0 0.7 tick.6
  28.8 0.7 collective-permute-start.9
  29.4 0.7 collective-permute-start.11
  30.1 0.7 collective-permute-start.10
  30.8 0.6 tick.7
  31.4 1.3 %collective-permute-start.12 = (bf16[4,160,128]{2,1,0:T(8,128)(2,1)S(1)}, bf16[4,160,128]{2,1,0:T(8,128)(2,1)S(1)}, u32[]{:S(2)}, u32[]{:S(2)}) collective-permute-start(bf16[4,160,128]{2,1,0:T(8,128)(2,1)S(1)} %get-tuple-element.42), channel_id=1, source_target_pairs={{16,24},{17,25},{18,26},{19,27},{20,28},{21,29},{22,30},{23,31},{8... | collective-permute-start | bytes 491528 | tf_op jit(solution)/shard_map/ppermute | solution.py:345
  32.7 1.3 %collective-permute-start.14 = (bf16[4,160,128]{2,1,0:T(8,128)(2,1)S(1)}, bf16[4,160,128]{2,1,0:T(8,128)(2,1)S(1)}, u32[]{:S(2)}, u32[]{:S(2)}) collective-permute-start(bf16[4,160,128]{2,1,0:T(8,128)(2,1)S(1)} %get-tuple-element.42), channel_id=1, source_target_pairs={{17,26},{19,28},{21,30},{18,25},{20,27},{22,29},{9,18},{11,20},{13... | collective-permute-start | bytes 491528 | tf_op jit(solution)/shard_map/ppermute | solution.py:345
  34.0 34.6 %collective-permute-done.12.refs_0_ = bf16[4,160,128]{2,1,0:T(8,128)(2,1)S(1)} collective-permute-done((bf16[4,160,128]{2,1,0:T(8,128)(2,1)S(1)}, bf16[4,160,128]{2,1,0:T(8,128)(2,1)S(1)}, u32[]{:S(2)}, u32[]{:S(2)}) %collective-permute-start.12) | collective-permute-done | bytes 163872 | tf_op jit(solution)/shard_map/ppermute | solution.py:345
  68.6 3.3 %collective-permute-start.13 = (bf16[4,160,128]{2,1,0:T(8,128)(2,1)S(1)}, bf16[4,160,128]{2,1,0:T(8,128)(2,1)S(1)}, u32[]{:S(2)}, u32[]{:S(2)}) collective-permute-start(bf16[4,160,128]{2,1,0:T(8,128)(2,1)S(1)} %collective-permute-done.12.refs_0_), channel_id=1, source_target_pairs={{24,25},{25,24},{26,27},{27,26},{28,29},{29,28},{30,31},{31,30},{1... | collective-permute-start | bytes 491528 | tf_op jit(solution)/shard_map/ppermute | solution.py:342
  71.9 1.0 %collective-permute-done.13.refs_1_ = bf16[4,160,128]{2,1,0:T(8,128)(2,1)S(1)} collective-permute-done((bf16[4,160,128]{2,1,0:T(8,128)(2,1)S(1)}, bf16[4,160,128]{2,1,0:T(8,128)(2,1)S(1)}, u32[]{:S(2)}, u32[]{:S(2)}) %collective-permute-start.13) | collective-permute-done | bytes 163872 | tf_op jit(solution)/shard_map/ppermute | solution.py:342
  72.9 4.7 %tick.8 = (bf16[4,160,128]{2,1,0:T(8,128)(2,1)S(1)}, bf16[4,12,160,128]{3,2,1,0:T(8,128)(2,1)S(1)}, bf16[2,4,160,128]{3,2,1,0:T(8,128)(2,1)}) custom-call(s32[3]{0:T(128)S(1)} %pad_add_fusion.flags, bf16[4,9,3,128,128]{4,3,2,1,0:T(8,128)(2,1)S(1)} %bitcast.11, f32[4,128]{1,0:T(4,128)S(1)} %bitcast.18, ...), custom_call_target="tpu_custom_call", output_to_operand_aliasing={{2}: (13, {})} | custom-call | flops 2642411520 | bytes 4000000 | tf_op jit(solution)/shard_map/tick/pallas_call | solution.py:310
  77.6 1.3 %collective-permute-start.15 = (bf16[4,160,128]{2,1,0:T(8,128)(2,1)S(1)}, bf16[4,160,128]{2,1,0:T(8,128)(2,1)S(1)}, u32[]{:S(2)}, u32[]{:S(2)}) collective-permute-start(bf16[4,160,128]{2,1,0:T(8,128)(2,1)S(1)} %get-tuple-element.45), channel_id=1, source_target_pairs={{16,24},{17,25},{18,26},{19,27},{20,28},{21,29},{22,30},{23,31}} | collective-permute-start | bytes 491528 | tf_op jit(solution)/shard_map/ppermute | solution.py:345
  78.9 1.3 %collective-permute-start.17 = (bf16[4,160,128]{2,1,0:T(8,128)(2,1)S(1)}, bf16[4,160,128]{2,1,0:T(8,128)(2,1)S(1)}, u32[]{:S(2)}, u32[]{:S(2)}) collective-permute-start(bf16[4,160,128]{2,1,0:T(8,128)(2,1)S(1)} %get-tuple-element.45), channel_id=1, source_target_pairs={{17,26},{19,28},{21,30},{18,25},{20,27},{22,29}} | collective-permute-start | bytes 491528 | tf_op jit(solution)/shard_map/ppermute | solution.py:345
  80.2 4.6 %collective-permute-done.15.refs_0_ = bf16[4,160,128]{2,1,0:T(8,128)(2,1)S(1)} collective-permute-done((bf16[4,160,128]{2,1,0:T(8,128)(2,1)S(1)}, bf16[4,160,128]{2,1,0:T(8,128)(2,1)S(1)}, u32[]{:S(2)}, u32[]{:S(2)}) %collective-permute-start.15) | collective-permute-done | bytes 163872 | tf_op jit(solution)/shard_map/ppermute | solution.py:345
  84.8 4.6 %collective-permute-start.16 = (bf16[4,160,128]{2,1,0:T(8,128)(2,1)S(1)}, bf16[4,160,128]{2,1,0:T(8,128)(2,1)S(1)}, u32[]{:S(2)}, u32[]{:S(2)}) collective-permute-start(bf16[4,160,128]{2,1,0:T(8,128)(2,1)S(1)} %collective-permute-done.15.refs_0_), channel_id=1, source_target_pairs={{24,25},{25,24},{26,27},{27,26},{28,29},{29,28},{30,31},{31,30}} | collective-permute-start | bytes 491528 | tf_op jit(solution)/shard_map/ppermute | solution.py:342
  89.5 1.0 %collective-permute-done.16.refs_1_ = bf16[4,160,128]{2,1,0:T(8,128)(2,1)S(1)} collective-permute-done((bf16[4,160,128]{2,1,0:T(8,128)(2,1)S(1)}, bf16[4,160,128]{2,1,0:T(8,128)(2,1)S(1)}, u32[]{:S(2)}, u32[]{:S(2)}) %collective-permute-start.16) | collective-permute-done | bytes 163872 | tf_op jit(solution)/shard_map/ppermute | solution.py:342
  90.5 4.6 %tick.9 = (bf16[4,160,128]{2,1,0:T(8,128)(2,1)}, bf16[2,4,160,128]{3,2,1,0:T(8,128)(2,1)}) custom-call(s32[3]{0:T(128)S(1)} %pad_add_fusion.flags, bf16[4,9,3,128,128]{4,3,2,1,0:T(8,128)(2,1)S(1)} %bitcast.12, f32[4,128]{1,0:T(4,128)S(1)} %bitcast.19, bf16[4,160,128]{2,1,0:T(8,128)(2,1)S(1)} %collective-permute-done.15.refs_0_, ...), custom_call_target="tpu_custom_call", output_to_operand_aliasing={{1}: (10, {})} | custom-call | flops 2642411520 | bytes 4000000 | tf_op jit(solution)/shard_map/tick/pallas_call | solution.py:310
  (20 shorter events, 0.0 us)
Async XLA Ops:
  0.0 11.2 %collective-permute-start.1 = (bf16[2,4,160,128]{3,2,1,0:T(8,128)(2,1)}, bf16[2,4,160,128]{3,2,1,0:T(8,128)(2,1)S(1)}, u32[]{:S(2)}, u32[]{:S(2)}) collective-permute-start(bf16[2,4,160,128]{3,2,1,0:T(8,128)(2,1)} %refs_0_.3), channel_id=1, source_target_pairs={{9,2},{11,4},{13,6},{10,1},{12,3},{14,5}} | collective-permute-start | bytes 983048 | tf_op jit(solution)/shard_map/ppermute | solution.py:349
  1.4 9.1 %copy-start.2 = (bf16[2,4,160,128]{3,2,1,0:T(8,128)(2,1)S(1)}, bf16[2,4,160,128]{3,2,1,0:T(8,128)(2,1)}, u32[]{:S(2)}) copy-start(bf16[2,4,160,128]{3,2,1,0:T(8,128)(2,1)} %refs_0_.3) | copy-start | bytes 983044
  1.4 9.8 %copy-start = (bf16[1,4,9,3,128,128]{5,4,3,2,1,0:T(8,128)(2,1)S(1)}, bf16[1,4,9,3,128,128]{5,4,3,2,1,0:T(8,128)(2,1)}, u32[]{:S(2)}) copy-start(bf16[1,4,9,3,128,128]{5,4,3,2,1,0:T(8,128)(2,1)} %param.7) | copy-start | bytes 10616836
  1.4 9.8 %copy-start.1 = (bf16[1,4,2,4,160,128]{5,4,3,2,1,0:T(8,128)(2,1)S(1)}, bf16[1,4,2,4,160,128]{5,4,3,2,1,0:T(8,128)(2,1)}, u32[]{:S(2)}) copy-start(bf16[1,4,2,4,160,128]{5,4,3,2,1,0:T(8,128)(2,1)} %param.6) | copy-start | bytes 3932164
  6.8 9.8 %collective-permute-start.2 = (bf16[10,160,128]{2,1,0:T(8,128)(2,1)S(1)}, bf16[10,160,128]{2,1,0:T(8,128)(2,1)S(1)}, u32[]{:S(2)}, u32[]{:S(2)}) collective-permute-start(bf16[10,160,128]{2,1,0:T(8,128)(2,1)S(1)} %get-tuple-element.29), channel_id=1, source_target_pairs={{0,1},{1,0},{2,3},{3,2},{4,5},{5,4},{6,7},{7,6},{8,9},{9,8},{10,11... | collective-permute-start | bytes 1228808 | tf_op jit(solution)/shard_map/ppermute | solution.py:342
  7.5 11.7 %collective-permute-start.3 = (bf16[10,160,128]{2,1,0:T(8,128)(2,1)S(1)}, bf16[10,160,128]{2,1,0:T(8,128)(2,1)S(1)}, u32[]{:S(2)}, u32[]{:S(2)}) collective-permute-start(bf16[10,160,128]{2,1,0:T(8,128)(2,1)S(1)} %get-tuple-element.30), channel_id=1, source_target_pairs={{1,2},{3,4},{5,6},{2,1},{4,3},{6,5},{9,10},{11,12},{13,14},{10,9},... | collective-permute-start | bytes 1228808 | tf_op jit(solution)/shard_map/ppermute | solution.py:342
  10.5 6.0 %collective-permute-start = (bf16[2,4,160,128]{3,2,1,0:T(8,128)(2,1)S(1)}, bf16[2,4,160,128]{3,2,1,0:T(8,128)(2,1)S(1)}, u32[]{:S(2)}, u32[]{:S(2)}) collective-permute-start(bf16[2,4,160,128]{3,2,1,0:T(8,128)(2,1)S(1)} %copy-done.2), channel_id=1, source_target_pairs={{0,1},{1,0},{2,3},{3,2},{4,5},{5,4},{6,7},{7,6}} | collective-permute-start | bytes 983048 | tf_op jit(solution)/shard_map/ppermute | solution.py:342
  11.3 8.0 %copy-start.3 = (f32[1,4,128]{2,1,0:T(4,128)S(1)}, f32[1,4,128]{2,1,0:T(4,128)}, u32[]{:S(2)}) copy-start(f32[1,4,128]{2,1,0:T(4,128)} %param.8) | copy-start | bytes 6148
  13.9 8.0 %collective-permute-start.7 = (bf16[10,160,128]{2,1,0:T(8,128)(2,1)S(1)}, bf16[10,160,128]{2,1,0:T(8,128)(2,1)S(1)}, u32[]{:S(2)}, u32[]{:S(2)}) collective-permute-start(bf16[10,160,128]{2,1,0:T(8,128)(2,1)S(1)} %get-tuple-element.35), channel_id=1, source_target_pairs={{0,1},{1,0},{2,3},{3,2},{4,5},{5,4},{6,7},{7,6},{8,9},{9,8},{10,11... | collective-permute-start | bytes 1228808 | tf_op jit(solution)/shard_map/ppermute | solution.py:342
  14.4 13.6 %collective-permute-start.8 = (bf16[10,160,128]{2,1,0:T(8,128)(2,1)S(1)}, bf16[10,160,128]{2,1,0:T(8,128)(2,1)S(1)}, u32[]{:S(2)}, u32[]{:S(2)}) collective-permute-start(bf16[10,160,128]{2,1,0:T(8,128)(2,1)S(1)} %get-tuple-element.36), channel_id=1, source_target_pairs={{1,2},{3,4},{5,6},{2,1},{4,3},{6,5},{9,10},{11,12},{13,14},{10,9},... | collective-permute-start | bytes 1228808 | tf_op jit(solution)/shard_map/ppermute | solution.py:342
  19.8 1.4 %collective-permute-start.4 = (bf16[4,160,128]{2,1,0:T(8,128)(2,1)S(1)}, bf16[4,160,128]{2,1,0:T(8,128)(2,1)S(1)}, u32[]{:S(2)}, u32[]{:S(2)}) collective-permute-start(bf16[4,160,128]{2,1,0:T(8,128)(2,1)S(1)} %get-tuple-element.32), channel_id=1, source_target_pairs={{0,8},{1,9},{2,10},{3,11},{4,12},{5,13},{6,14},{7,15}} | collective-permute-start | bytes 491528 | tf_op jit(solution)/shard_map/ppermute | solution.py:345
  20.5 1.4 %collective-permute-start.6 = (bf16[4,160,128]{2,1,0:T(8,128)(2,1)S(1)}, bf16[4,160,128]{2,1,0:T(8,128)(2,1)S(1)}, u32[]{:S(2)}, u32[]{:S(2)}) collective-permute-start(bf16[4,160,128]{2,1,0:T(8,128)(2,1)S(1)} %get-tuple-element.32), channel_id=1, source_target_pairs={{1,10},{3,12},{5,14},{2,9},{4,11},{6,13}} | collective-permute-start | bytes 491528 | tf_op jit(solution)/shard_map/ppermute | solution.py:345
  21.2 0.7 collective-permute-start.5
  28.8 1.4 %collective-permute-start.9 = (bf16[4,160,128]{2,1,0:T(8,128)(2,1)S(1)}, bf16[4,160,128]{2,1,0:T(8,128)(2,1)S(1)}, u32[]{:S(2)}, u32[]{:S(2)}) collective-permute-start(bf16[4,160,128]{2,1,0:T(8,128)(2,1)S(1)} %get-tuple-element.39), channel_id=1, source_target_pairs={{8,16},{9,17},{10,18},{11,19},{12,20},{13,21},{14,22},{15,23},{0,8... | collective-permute-start | bytes 491528 | tf_op jit(solution)/shard_map/ppermute | solution.py:345
  29.4 1.4 %collective-permute-start.11 = (bf16[4,160,128]{2,1,0:T(8,128)(2,1)S(1)}, bf16[4,160,128]{2,1,0:T(8,128)(2,1)S(1)}, u32[]{:S(2)}, u32[]{:S(2)}) collective-permute-start(bf16[4,160,128]{2,1,0:T(8,128)(2,1)S(1)} %get-tuple-element.39), channel_id=1, source_target_pairs={{9,18},{11,20},{13,22},{10,17},{12,19},{14,21},{1,10},{3,12},{5,14... | collective-permute-start | bytes 491528 | tf_op jit(solution)/shard_map/ppermute | solution.py:345
  30.1 0.7 collective-permute-start.10
  31.4 37.2 %collective-permute-start.12 = (bf16[4,160,128]{2,1,0:T(8,128)(2,1)S(1)}, bf16[4,160,128]{2,1,0:T(8,128)(2,1)S(1)}, u32[]{:S(2)}, u32[]{:S(2)}) collective-permute-start(bf16[4,160,128]{2,1,0:T(8,128)(2,1)S(1)} %get-tuple-element.42), channel_id=1, source_target_pairs={{16,24},{17,25},{18,26},{19,27},{20,28},{21,29},{22,30},{23,31},{8... | collective-permute-start | bytes 491528 | tf_op jit(solution)/shard_map/ppermute | solution.py:345
  32.7 39.1 %collective-permute-start.14 = (bf16[4,160,128]{2,1,0:T(8,128)(2,1)S(1)}, bf16[4,160,128]{2,1,0:T(8,128)(2,1)S(1)}, u32[]{:S(2)}, u32[]{:S(2)}) collective-permute-start(bf16[4,160,128]{2,1,0:T(8,128)(2,1)S(1)} %get-tuple-element.42), channel_id=1, source_target_pairs={{17,26},{19,28},{21,30},{18,25},{20,27},{22,29},{9,18},{11,20},{13... | collective-permute-start | bytes 491528 | tf_op jit(solution)/shard_map/ppermute | solution.py:345
  68.6 4.3 %collective-permute-start.13 = (bf16[4,160,128]{2,1,0:T(8,128)(2,1)S(1)}, bf16[4,160,128]{2,1,0:T(8,128)(2,1)S(1)}, u32[]{:S(2)}, u32[]{:S(2)}) collective-permute-start(bf16[4,160,128]{2,1,0:T(8,128)(2,1)S(1)} %collective-permute-done.12.refs_0_), channel_id=1, source_target_pairs={{24,25},{25,24},{26,27},{27,26},{28,29},{29,28},{30,31},{31,30},{1... | collective-permute-start | bytes 491528 | tf_op jit(solution)/shard_map/ppermute | solution.py:342
  77.6 7.2 %collective-permute-start.15 = (bf16[4,160,128]{2,1,0:T(8,128)(2,1)S(1)}, bf16[4,160,128]{2,1,0:T(8,128)(2,1)S(1)}, u32[]{:S(2)}, u32[]{:S(2)}) collective-permute-start(bf16[4,160,128]{2,1,0:T(8,128)(2,1)S(1)} %get-tuple-element.45), channel_id=1, source_target_pairs={{16,24},{17,25},{18,26},{19,27},{20,28},{21,29},{22,30},{23,31}} | collective-permute-start | bytes 491528 | tf_op jit(solution)/shard_map/ppermute | solution.py:345
  78.9 10.6 %collective-permute-start.17 = (bf16[4,160,128]{2,1,0:T(8,128)(2,1)S(1)}, bf16[4,160,128]{2,1,0:T(8,128)(2,1)S(1)}, u32[]{:S(2)}, u32[]{:S(2)}) collective-permute-start(bf16[4,160,128]{2,1,0:T(8,128)(2,1)S(1)} %get-tuple-element.45), channel_id=1, source_target_pairs={{17,26},{19,28},{21,30},{18,25},{20,27},{22,29}} | collective-permute-start | bytes 491528 | tf_op jit(solution)/shard_map/ppermute | solution.py:345
  84.8 5.6 %collective-permute-start.16 = (bf16[4,160,128]{2,1,0:T(8,128)(2,1)S(1)}, bf16[4,160,128]{2,1,0:T(8,128)(2,1)S(1)}, u32[]{:S(2)}, u32[]{:S(2)}) collective-permute-start(bf16[4,160,128]{2,1,0:T(8,128)(2,1)S(1)} %collective-permute-done.15.refs_0_), channel_id=1, source_target_pairs={{24,25},{25,24},{26,27},{27,26},{28,29},{29,28},{30,31},{31,30}} | collective-permute-start | bytes 491528 | tf_op jit(solution)/shard_map/ppermute | solution.py:342
where the time goes:
time: 93.7 us; the launch traced here: 95.3 us
  waiting for transfers between devices  50 us (53%)
  starting transfers between devices  24.8 us (26%)
  Pallas kernels  19.2 us (20%)
  between operations  1.14 us (1%)
    ppermute x8, waiting for transfers between devices, ahead(): lax.ppermute(value, axes, [(s * bands + a, (s + 1) * bands + b) for s in...  39.2 us
    ppermute x9, starting transfers between devices, swap(): lax.ppermute(value, axes, [(s * bands + a, s * bands + b) for s in chosen...  16.3 us
    pallas_call x5, Pallas kernels, tick_call(): pl.pallas_call(functools.partial(tick_kernel, tick, segments, bands), out...  11.2 us
    ppermute x9, waiting for transfers between devices, swap(): lax.ppermute(value, axes, [(s * bands + a, s * bands + b) for s in chosen...  10.8 us
    pallas_call x2, Pallas kernels, history_call(): pl.pallas_call(functools.partial(history_kernel, frame), out_shape=tuple(...  7.99 us
    ppermute x8, starting transfers between devices, ahead(): lax.ppermute(value, axes, [(s * bands + a, (s + 1) * bands + b) for s in...  7.85 us
  transfers between devices with their start and end apart: 18, of which 6 were waited for; matrix products, arithmetic and copies ran while one was open for 0% of the time, Pallas kernels for 9%

commit v1 on v0

--- a/solution.py
+++ b/solution.py
@@ -78,7 +78,7 @@
     layers, _, rows, width, channels = caches.shape
     begin = layers - flags[2]
     if frame == 0:
-        done, held, wb, s, lines, sems = refs
+        held, wb, s, lines, sems = refs
     else:
         held, wb = caches, w
         s, lines = refs
@@ -159,11 +159,11 @@
     sums0 = take(3) if zero else None
     sums1 = take(3) if one else None
     behind = take(1)[0] if one else None
-    done = take(1)
-    x_out = take(1)[0]
+    results = take(segments) if not zero else []
+    out = take(1)[0]
     ahead = take(1)[0] if zero else None
-    done_out, x, s, lines, part, sem = refs
-    rows, width, channels = x_out.shape
+    x, s, lines, part, sems = refs
+    rows, width, channels = out.shape[-3:]
     layers = w.shape[0]
     starts = message_starts(layers)
     band = flags[1]
@@ -237,10 +237,25 @@
                         known = known + behind[level, at : at + step].astype(F32)
                     x[at : at + step] = (x[at : at + step].astype(F32) + (mine + known)).astype(BF16)
 
-        copy = pltpu.make_async_copy(x.at[rows : 2 * rows], done_out.at[frame], sem)
-        copy.start()
-        x_out[...] = x[rows : 2 * rows]
-        copy.wait()
+        if zero:
+            out[...] = x[rows : 2 * rows]
+        else:
+            copy = pltpu.make_async_copy(x.at[rows : 2 * rows], out.at[frame], sems.at[1])
+            copy.start()
+            copy.wait()
+
+    def finished(section):
+        count = 2 if section + 1 < segments else 1
+        return [
+            pltpu.make_async_copy(results[section + f], out.at[f], sems.at[f]) for f in range(count)
+        ]
+
+    for section in range(len(results)):
+
+        @pl.when(flags[0] == section)
+        def _(section=section):
+            for copy in finished(section):
+                copy.start()
 
     for frame, present, parts in ((0, zero, sums0), (1, one, sums1)):
         if present:
@@ -249,6 +264,13 @@
             @pl.when(flags[0] == tick - frame)
             def _(frame=frame, fresh=fresh, parts=parts):
                 run(frame, fresh, *(clip if fresh else (own, inner, cross)), parts[0], parts[1:])
+
+    for section in range(len(results)):
+
+        @pl.when(flags[0] == section)
+        def _(section=section):
+            for copy in finished(section):
+                copy.wait()
 
 
 def in_vmem(count):
@@ -271,8 +293,6 @@
     specs = in_vmem(3)
     scratch = [pltpu.VMEM((2, rows + 4, width, 3 * channels), BF16), pltpu.VMEM((2, width + 2 * PAD, channels), F32)]
     if frame == 0:
-        outs.append(jax.ShapeDtypeStruct((2, rows) + row, BF16))
-        specs.append(anywhere())
         scratch = [
             pltpu.VMEM(caches.shape, BF16),
             pltpu.VMEM((layers, 9, 2, channels, channels), BF16),
@@ -294,38 +314,38 @@
     )(flags, caches, weights)
 
 
-def tick_call(tick, segments, bands, flags, clip, received, weights, biases, sums0, sums1, behind, done):
+def tick_call(tick, segments, bands, flags, clip, received, weights, biases, sums0, sums1, behind, results):
     layers, _, _, channels, _ = weights.shape
-    rows, width = done.shape[1:3]
+    rows, width = clip[0].shape[1:3]
     every = (layers, 3 * rows, width, channels)
     pixels = sum(rows + 2 * level for level in range(layers)) * width
     zero, one = tick < segments, tick > 0
     extra = (list(clip) if tick < 2 else []) + (list(received) if one else [])
     extra += (list(sums0) if zero else []) + (list(sums1) + [behind] if one else [])
-    outs = [jax.ShapeDtypeStruct((rows, width, channels), BF16)]
     if zero:
-        outs.append(jax.ShapeDtypeStruct(every, BF16))
-    specs = in_vmem(len(outs)) + [anywhere()]
-    outs.append(jax.ShapeDtypeStruct(done.shape, BF16))
+        outs = [jax.ShapeDtypeStruct((rows, width, channels), BF16), jax.ShapeDtypeStruct(every, BF16)]
+        specs = in_vmem(2)
+    else:
+        extra += results
+        outs, specs = [jax.ShapeDtypeStruct(clip[0].shape, BF16)], [anywhere()]
     return pl.pallas_call(
         functools.partial(tick_kernel, tick, segments, bands),
         out_shape=tuple(outs),
-        in_specs=[in_smem()] + in_vmem(2 + len(extra)) + [anywhere()],
+        in_specs=[in_smem()] + in_vmem(2 + len(extra)),
         out_specs=tuple(specs),
         scratch_shapes=[
             pltpu.VMEM((3 * rows, width, channels), BF16),
             pltpu.VMEM((3 * rows, width, 3 * channels), BF16),
             pltpu.VMEM((2, width + 2 * PAD, channels), F32),
             pltpu.VMEM(every, BF16),
-            pltpu.SemaphoreType.DMA,
+            pltpu.SemaphoreType.DMA((2,)),
         ],
-        input_output_aliases={3 + len(extra): len(outs) - 1},
         compiler_params=pltpu.CompilerParams(vmem_limit_bytes=LIMIT),
         cost_estimate=pl.CostEstimate(
             flops=pixels * 18 * 2 * channels * channels, bytes_accessed=4000000, transcendentals=pixels * channels
         ),
         name="tick",
-    )(flags, weights, biases, *extra, done)
+    )(flags, weights, biases, *extra)
 
 
 def per_device(clip, caches, weights, biases, section_layers):
@@ -351,23 +371,25 @@
     everyone = range(segments)
     clip_cross = lender(clip, between)
     clip_in = swap(clip, in_chip, [0])
-    sums, inner, cross, done = history_call(0, flags, caches, weights)
+    sums, inner, cross = history_call(0, flags, caches, weights)
     sums0 = (sums, swap(inner, in_chip, everyone), swap(cross, between, everyone))
     caches, clip_cross, _ = lax.optimization_barrier((caches, clip_cross, sums))
     sums, inner, cross = history_call(1, flags, caches, weights)
     sums1 = (sums, swap(inner, in_chip, everyone), swap(cross, between, everyone))
     halves = (clip, clip_in, clip_cross)
     received = behind = None
+    results = []
     for tick in range(segments + 1):
-        x, *later, done = tick_call(
-            tick, segments, bands, flags, halves, received, weights, biases, sums0, sums1, behind, done
+        x, *later = tick_call(
+            tick, segments, bands, flags, halves, received, weights, biases, sums0, sums1, behind, results
         )
         if tick < segments:
             (behind,) = later
+            results.append(x)
             sources = [s for s in (tick, tick - 1) if 0 <= s < segments - 1]
             own, cross = ahead(x, straight, sources), ahead(x, between, sources)
             received = (own, swap(own, in_chip, [s + 1 for s in sources]), cross)
-    return done[None]
+    return x[None]
 
 
 def solution(mesh):

time: 93.7 us -> 88 us (0.939)
  Pallas kernels: 19.2 us -> 9.98 us
  waiting for transfers between devices: 50 us -> 54.2 us
  starting transfers between devices: 24.8 us -> 23.4 us
    pallas_call x5, Pallas kernels: 11.2 us -> 5.58 us  [tick_call(): pl.pallas_call(functools.partial(tick_kernel, tick, segments, bands), out...]
    pallas_call x2, Pallas kernels: 7.99 us -> 4.4 us  [history_call(): pl.pallas_call(functools.partial(history_kernel, frame), out_shape=tuple(...]
    ppermute x8, waiting for transfers between devices: 39.2 us -> 42.1 us  [ahead(): lax.ppermute(value, axes, [(s * bands + a, (s + 1) * bands + b) for s in...]
    ppermute x9, starting transfers between devices: 16.3 us -> 14.9 us  [swap(): lax.ppermute(value, axes, [(s * bands + a, s * bands + b) for s in chosen...]
    ppermute x9, waiting for transfers between devices: 10.8 us -> 12.1 us  [swap(): lax.ppermute(value, axes, [(s * bands + a, s * bands + b) for s in chosen...]
  transfers between devices with their start and end apart: 18 -> 18, of which waited for: 6 -> 6; matrix products, arithmetic and copies ran while one was open for 0% -> 0% of each run, Pallas kernels for 9% -> 6%
where the time goes in v1:
time: 88 us; the launch traced here: 88.8 us
  waiting for transfers between devices  54.2 us (62%)
  starting transfers between devices  23.4 us (27%)
  Pallas kernels  9.98 us (11%)
  between operations  1.14 us (1%)
    ppermute x8, waiting for transfers between devices, ahead(): lax.ppermute(value, axes, [(s * bands + a, (s + 1) * bands + b) for s in...  42.1 us
    ppermute x9, starting transfers between devices, swap(): lax.ppermute(value, axes, [(s * bands + a, s * bands + b) for s in chosen...  14.9 us
    ppermute x9, waiting for transfers between devices, swap(): lax.ppermute(value, axes, [(s * bands + a, s * bands + b) for s in chosen...  12.1 us
    ppermute x8, starting transfers between devices, ahead(): lax.ppermute(value, axes, [(s * bands + a, (s + 1) * bands + b) for s in...  7.85 us
    pallas_call x5, Pallas kernels, tick_call(): pl.pallas_call(functools.partial(tick_kernel, tick, segments, bands), out...  5.58 us
    pallas_call x2, Pallas kernels, history_call(): pl.pallas_call(functools.partial(history_kernel, frame), out_shape=tuple(...  4.4 us
  transfers between devices with their start and end apart: 18, of which 6 were waited for; matrix products, arithmetic and copies ran while one was open for 0% of the time, Pallas kernels for 6%

profile of v1, /device:TPU:29, one launch (start us, length us, event | category | flops | bytes accessed | tf_op | source)
XLA Modules:
  0.0 88.8 jit_solution(630969554071322760)
XLA Ops:
  0.0 0.7 collective-permute-start.1
  1.3 0.1 pad_add_fusion.flags
  1.4 3.1 %history.2 = (bf16[4,6,160,128]{3,2,1,0:T(8,128)(2,1)S(1)}, bf16[10,160,128]{2,1,0:T(8,128)(2,1)S(1)}, bf16[10,160,128]{2,1,0:T(8,128)(2,1)S(1)}) custom-call(s32[3]{0:T(128)S(1)} %pad_add_fusion.flags, bf16[4,2,4,160,128]{4,3,2,1,0:T(8,128)(2,1)} %bitcast.13, bf16[4,9,3,128,128]{4,3,2,1,0:T(8,128)(2,1)} %bitcast.6), custom_call_target="tpu_custom_call" | custom-call | flops 2264924160 | bytes 4000000 | tf_op jit(solution)/shard_map/history/pallas_call | solution.py:303
  4.5 0.7 collective-permute-start.2
  5.2 3.0 %collective-permute-start.3 = (bf16[10,160,128]{2,1,0:T(8,128)(2,1)S(1)}, bf16[10,160,128]{2,1,0:T(8,128)(2,1)S(1)}, u32[]{:S(2)}, u32[]{:S(2)}) collective-permute-start(bf16[10,160,128]{2,1,0:T(8,128)(2,1)S(1)} %get-tuple-element.24), channel_id=1, source_target_pairs={{1,2},{3,4},{5,6},{2,1},{4,3},{6,5},{9,10},{11,12},{13,14},{10,9},... | collective-permute-start | bytes 1228808 | tf_op jit(solution)/shard_map/ppermute | solution.py:362
  8.3 0.7 collective-permute-start
  9.0 1.3 %history.3 = (bf16[4,6,160,128]{3,2,1,0:T(8,128)(2,1)S(1)}, bf16[10,160,128]{2,1,0:T(8,128)(2,1)S(1)}, bf16[10,160,128]{2,1,0:T(8,128)(2,1)S(1)}) custom-call(s32[3]{0:T(128)S(1)} %pad_add_fusion.flags, bf16[4,2,4,160,128]{4,3,2,1,0:T(8,128)(2,1)S(1)} %bitcast.14, bf16[4,9,3,128,128]{4,3,2,1,0:T(8,128)(2,1)S(1)} %bitcast.7), custom_call_target="tpu_custom_call" | custom-call | flops 1132462080 | bytes 4000000 | tf_op jit(solution)/shard_map/history/pallas_call | solution.py:303
  10.3 0.5 collective-permute-start.7
  10.8 2.1 %collective-permute-start.8 = (bf16[10,160,128]{2,1,0:T(8,128)(2,1)S(1)}, bf16[10,160,128]{2,1,0:T(8,128)(2,1)S(1)}, u32[]{:S(2)}, u32[]{:S(2)}) collective-permute-start(bf16[10,160,128]{2,1,0:T(8,128)(2,1)S(1)} %get-tuple-element.29), channel_id=1, source_target_pairs={{1,2},{3,4},{5,6},{2,1},{4,3},{6,5},{9,10},{11,12},{13,14},{10,9},... | collective-permute-start | bytes 1228808 | tf_op jit(solution)/shard_map/ppermute | solution.py:362
  13.0 4.0 %collective-permute-done.3.refs_5_.refs_8_ = bf16[10,160,128]{2,1,0:T(8,128)(2,1)S(1)} collective-permute-done((bf16[10,160,128]{2,1,0:T(8,128)(2,1)S(1)}, bf16[10,160,128]{2,1,0:T(8,128)(2,1)S(1)}, u32[]{:S(2)}, u32[]{:S(2)}) %collective-permute-start.3) | collective-permute-done | bytes 409632 | tf_op jit(solution)/shard_map/ppermute | solution.py:362
  17.0 0.6 tick.5
  17.5 0.7 collective-permute-start.4
  18.2 0.7 collective-permute-start.6
  18.9 0.7 collective-permute-start.5
  19.6 6.1 %collective-permute-done.8.refs_11_.refs_8_.refs_5_ = bf16[10,160,128]{2,1,0:T(8,128)(2,1)S(1)} collective-permute-done((bf16[10,160,128]{2,1,0:T(8,128)(2,1)S(1)}, bf16[10,160,128]{2,1,0:T(8,128)(2,1)S(1)}, u32[]{:S(2)}, u32[]{:S(2)}) %collective-permute-start.8) | collective-permute-done | bytes 409632 | tf_op jit(solution)/shard_map/ppermute | solution.py:362
  25.7 0.8 tick.6
  26.5 0.7 collective-permute-start.9
  27.2 0.7 collective-permute-start.11
  27.9 0.7 collective-permute-start.10
  28.6 0.6 tick.7
  29.2 1.3 %collective-permute-start.12 = (bf16[4,160,128]{2,1,0:T(8,128)(2,1)S(1)}, bf16[4,160,128]{2,1,0:T(8,128)(2,1)S(1)}, u32[]{:S(2)}, u32[]{:S(2)}) collective-permute-start(bf16[4,160,128]{2,1,0:T(8,128)(2,1)S(1)} %get-tuple-element.33.refs_9_), channel_id=1, source_target_pairs={{16,24},{17,25},{18,26},{19,27},{20,28},{21,29},{22,30},{23,31},{8... | collective-permute-start | bytes 491528 | tf_op jit(solution)/shard_map/ppermute | solution.py:365
  30.5 1.3 %collective-permute-start.14 = (bf16[4,160,128]{2,1,0:T(8,128)(2,1)S(1)}, bf16[4,160,128]{2,1,0:T(8,128)(2,1)S(1)}, u32[]{:S(2)}, u32[]{:S(2)}) collective-permute-start(bf16[4,160,128]{2,1,0:T(8,128)(2,1)S(1)} %get-tuple-element.33.refs_9_), channel_id=1, source_target_pairs={{17,26},{19,28},{21,30},{18,25},{20,27},{22,29},{9,18},{11,20},{13... | collective-permute-start | bytes 491528 | tf_op jit(solution)/shard_map/ppermute | solution.py:365
  31.8 34.2 %collective-permute-done.12.refs_0_ = bf16[4,160,128]{2,1,0:T(8,128)(2,1)S(1)} collective-permute-done((bf16[4,160,128]{2,1,0:T(8,128)(2,1)S(1)}, bf16[4,160,128]{2,1,0:T(8,128)(2,1)S(1)}, u32[]{:S(2)}, u32[]{:S(2)}) %collective-permute-start.12) | collective-permute-done | bytes 163872 | tf_op jit(solution)/shard_map/ppermute | solution.py:365
  65.9 3.2 %collective-permute-start.13 = (bf16[4,160,128]{2,1,0:T(8,128)(2,1)S(1)}, bf16[4,160,128]{2,1,0:T(8,128)(2,1)S(1)}, u32[]{:S(2)}, u32[]{:S(2)}) collective-permute-start(bf16[4,160,128]{2,1,0:T(8,128)(2,1)S(1)} %collective-permute-done.12.refs_0_), channel_id=1, source_target_pairs={{24,25},{25,24},{26,27},{27,26},{28,29},{29,28},{30,31},{31,30},{1... | collective-permute-start | bytes 491528 | tf_op jit(solution)/shard_map/ppermute | solution.py:362
  69.2 1.0 %collective-permute-done.13.refs_1_ = bf16[4,160,128]{2,1,0:T(8,128)(2,1)S(1)} collective-permute-done((bf16[4,160,128]{2,1,0:T(8,128)(2,1)S(1)}, bf16[4,160,128]{2,1,0:T(8,128)(2,1)S(1)}, u32[]{:S(2)}, u32[]{:S(2)}) %collective-permute-start.13) | collective-permute-done | bytes 163872 | tf_op jit(solution)/shard_map/ppermute | solution.py:362
  70.2 1.7 %tick.8 = (bf16[4,160,128]{2,1,0:T(8,128)(2,1)S(1)}, bf16[4,12,160,128]{3,2,1,0:T(8,128)(2,1)S(1)}) custom-call(s32[3]{0:T(128)S(1)} %pad_add_fusion.flags, bf16[4,9,3,128,128]{4,3,2,1,0:T(8,128)(2,1)S(1)} %bitcast.11, f32[4,128]{1,0:T(4,128)S(1)} %bitcast.18, bf16[4,160,128]{2,1,0:T(8,128)(2,1)S(1)} %collective-permute-done.12.refs_0_, ...), custom_call_target="tpu_custom_call" | custom-call | flops 2642411520 | bytes 4000000 | tf_op jit(solution)/shard_map/tick/pallas_call | solution.py:331
  71.9 1.3 %collective-permute-start.15 = (bf16[4,160,128]{2,1,0:T(8,128)(2,1)S(1)}, bf16[4,160,128]{2,1,0:T(8,128)(2,1)S(1)}, u32[]{:S(2)}, u32[]{:S(2)}) collective-permute-start(bf16[4,160,128]{2,1,0:T(8,128)(2,1)S(1)} %get-tuple-element.35.refs_10_), channel_id=1, source_target_pairs={{16,24},{17,25},{18,26},{19,27},{20,28},{21,29},{22,30},{23,31}} | collective-permute-start | bytes 491528 | tf_op jit(solution)/shard_map/ppermute | solution.py:365
  73.2 1.3 %collective-permute-start.17 = (bf16[4,160,128]{2,1,0:T(8,128)(2,1)S(1)}, bf16[4,160,128]{2,1,0:T(8,128)(2,1)S(1)}, u32[]{:S(2)}, u32[]{:S(2)}) collective-permute-start(bf16[4,160,128]{2,1,0:T(8,128)(2,1)S(1)} %get-tuple-element.35.refs_10_), channel_id=1, source_target_pairs={{17,26},{19,28},{21,30},{18,25},{20,27},{22,29}} | collective-permute-start | bytes 491528 | tf_op jit(solution)/shard_map/ppermute | solution.py:365
  74.5 7.9 %collective-permute-done.15.refs_0_ = bf16[4,160,128]{2,1,0:T(8,128)(2,1)S(1)} collective-permute-done((bf16[4,160,128]{2,1,0:T(8,128)(2,1)S(1)}, bf16[4,160,128]{2,1,0:T(8,128)(2,1)S(1)}, u32[]{:S(2)}, u32[]{:S(2)}) %collective-permute-start.15) | collective-permute-done | bytes 163872 | tf_op jit(solution)/shard_map/ppermute | solution.py:365
  82.4 3.3 %collective-permute-start.16 = (bf16[4,160,128]{2,1,0:T(8,128)(2,1)S(1)}, bf16[4,160,128]{2,1,0:T(8,128)(2,1)S(1)}, u32[]{:S(2)}, u32[]{:S(2)}) collective-permute-start(bf16[4,160,128]{2,1,0:T(8,128)(2,1)S(1)} %collective-permute-done.15.refs_0_), channel_id=1, source_target_pairs={{24,25},{25,24},{26,27},{27,26},{28,29},{29,28},{30,31},{31,30}} | collective-permute-start | bytes 491528 | tf_op jit(solution)/shard_map/ppermute | solution.py:362
  85.7 1.0 %collective-permute-done.16.refs_1_ = bf16[4,160,128]{2,1,0:T(8,128)(2,1)S(1)} collective-permute-done((bf16[4,160,128]{2,1,0:T(8,128)(2,1)S(1)}, bf16[4,160,128]{2,1,0:T(8,128)(2,1)S(1)}, u32[]{:S(2)}, u32[]{:S(2)}) %collective-permute-start.16) | collective-permute-done | bytes 163872 | tf_op jit(solution)/shard_map/ppermute | solution.py:362
  86.7 2.0 %tick.9 = bf16[2,4,160,128]{3,2,1,0:T(8,128)(2,1)} custom-call(s32[3]{0:T(128)S(1)} %pad_add_fusion.flags, bf16[4,9,3,128,128]{4,3,2,1,0:T(8,128)(2,1)S(1)} %bitcast.12, f32[4,128]{1,0:T(4,128)S(1)} %bitcast.19, bf16[4,160,128]{2,1,0:T(8,128)(2,1)S(1)} %collective-permute-done.15.refs_0_, bf16[4,160,128]{2,1,0:T(8,128)(2,1)S(1)} %collective-permute-done.16.refs_1_, ...), custom_call_target="tpu_custom_call" | custom-call | flops 2642411520 | bytes 4000000 | tf_op jit(solution)/shard_map/tick/pallas_call | solution.py:331
  (20 shorter events, 0.0 us)
Async XLA Ops:
  0.0 9.0 %collective-permute-start.1 = (bf16[2,4,160,128]{3,2,1,0:T(8,128)(2,1)}, bf16[2,4,160,128]{3,2,1,0:T(8,128)(2,1)S(1)}, u32[]{:S(2)}, u32[]{:S(2)}) collective-permute-start(bf16[2,4,160,128]{3,2,1,0:T(8,128)(2,1)} %refs_0_.3), channel_id=1, source_target_pairs={{9,2},{11,4},{13,6},{10,1},{12,3},{14,5}} | collective-permute-start | bytes 983048 | tf_op jit(solution)/shard_map/ppermute | solution.py:369
  1.4 6.9 %copy-start.2 = (bf16[2,4,160,128]{3,2,1,0:T(8,128)(2,1)S(1)}, bf16[2,4,160,128]{3,2,1,0:T(8,128)(2,1)}, u32[]{:S(2)}) copy-start(bf16[2,4,160,128]{3,2,1,0:T(8,128)(2,1)} %refs_0_.3) | copy-start | bytes 983044
  1.4 7.6 %copy-start = (bf16[1,4,9,3,128,128]{5,4,3,2,1,0:T(8,128)(2,1)S(1)}, bf16[1,4,9,3,128,128]{5,4,3,2,1,0:T(8,128)(2,1)}, u32[]{:S(2)}) copy-start(bf16[1,4,9,3,128,128]{5,4,3,2,1,0:T(8,128)(2,1)} %param.7) | copy-start | bytes 10616836
  1.4 7.6 %copy-start.1 = (bf16[1,4,2,4,160,128]{5,4,3,2,1,0:T(8,128)(2,1)S(1)}, bf16[1,4,2,4,160,128]{5,4,3,2,1,0:T(8,128)(2,1)}, u32[]{:S(2)}) copy-start(bf16[1,4,2,4,160,128]{5,4,3,2,1,0:T(8,128)(2,1)} %param.6) | copy-start | bytes 3932164
  4.5 8.5 %collective-permute-start.2 = (bf16[10,160,128]{2,1,0:T(8,128)(2,1)S(1)}, bf16[10,160,128]{2,1,0:T(8,128)(2,1)S(1)}, u32[]{:S(2)}, u32[]{:S(2)}) collective-permute-start(bf16[10,160,128]{2,1,0:T(8,128)(2,1)S(1)} %get-tuple-element.23), channel_id=1, source_target_pairs={{0,1},{1,0},{2,3},{3,2},{4,5},{5,4},{6,7},{7,6},{8,9},{9,8},{10,11... | collective-permute-start | bytes 1228808 | tf_op jit(solution)/shard_map/ppermute | solution.py:362
  5.2 11.7 %collective-permute-start.3 = (bf16[10,160,128]{2,1,0:T(8,128)(2,1)S(1)}, bf16[10,160,128]{2,1,0:T(8,128)(2,1)S(1)}, u32[]{:S(2)}, u32[]{:S(2)}) collective-permute-start(bf16[10,160,128]{2,1,0:T(8,128)(2,1)S(1)} %get-tuple-element.24), channel_id=1, source_target_pairs={{1,2},{3,4},{5,6},{2,1},{4,3},{6,5},{9,10},{11,12},{13,14},{10,9},... | collective-permute-start | bytes 1228808 | tf_op jit(solution)/shard_map/ppermute | solution.py:362
  8.3 4.7 %collective-permute-start = (bf16[2,4,160,128]{3,2,1,0:T(8,128)(2,1)S(1)}, bf16[2,4,160,128]{3,2,1,0:T(8,128)(2,1)S(1)}, u32[]{:S(2)}, u32[]{:S(2)}) collective-permute-start(bf16[2,4,160,128]{3,2,1,0:T(8,128)(2,1)S(1)} %copy-done.2), channel_id=1, source_target_pairs={{0,1},{1,0},{2,3},{3,2},{4,5},{5,4},{6,7},{7,6}} | collective-permute-start | bytes 983048 | tf_op jit(solution)/shard_map/ppermute | solution.py:362
  9.0 8.0 %copy-start.3 = (f32[1,4,128]{2,1,0:T(4,128)S(1)}, f32[1,4,128]{2,1,0:T(4,128)}, u32[]{:S(2)}) copy-start(f32[1,4,128]{2,1,0:T(4,128)} %param.8) | copy-start | bytes 6148
  10.3 9.3 %collective-permute-start.7 = (bf16[10,160,128]{2,1,0:T(8,128)(2,1)S(1)}, bf16[10,160,128]{2,1,0:T(8,128)(2,1)S(1)}, u32[]{:S(2)}, u32[]{:S(2)}) collective-permute-start(bf16[10,160,128]{2,1,0:T(8,128)(2,1)S(1)} %get-tuple-element.28), channel_id=1, source_target_pairs={{0,1},{1,0},{2,3},{3,2},{4,5},{5,4},{6,7},{7,6},{8,9},{9,8},{10,11... | collective-permute-start | bytes 1228808 | tf_op jit(solution)/shard_map/ppermute | solution.py:362
  10.8 14.9 %collective-permute-start.8 = (bf16[10,160,128]{2,1,0:T(8,128)(2,1)S(1)}, bf16[10,160,128]{2,1,0:T(8,128)(2,1)S(1)}, u32[]{:S(2)}, u32[]{:S(2)}) collective-permute-start(bf16[10,160,128]{2,1,0:T(8,128)(2,1)S(1)} %get-tuple-element.29), channel_id=1, source_target_pairs={{1,2},{3,4},{5,6},{2,1},{4,3},{6,5},{9,10},{11,12},{13,14},{10,9},... | collective-permute-start | bytes 1228808 | tf_op jit(solution)/shard_map/ppermute | solution.py:362
  17.5 1.4 %collective-permute-start.4 = (bf16[4,160,128]{2,1,0:T(8,128)(2,1)S(1)}, bf16[4,160,128]{2,1,0:T(8,128)(2,1)S(1)}, u32[]{:S(2)}, u32[]{:S(2)}) collective-permute-start(bf16[4,160,128]{2,1,0:T(8,128)(2,1)S(1)} %get-tuple-element.25.refs_7_), channel_id=1, source_target_pairs={{0,8},{1,9},{2,10},{3,11},{4,12},{5,13},{6,14},{7,15}} | collective-permute-start | bytes 491528 | tf_op jit(solution)/shard_map/ppermute | solution.py:365
  18.2 1.4 %collective-permute-start.6 = (bf16[4,160,128]{2,1,0:T(8,128)(2,1)S(1)}, bf16[4,160,128]{2,1,0:T(8,128)(2,1)S(1)}, u32[]{:S(2)}, u32[]{:S(2)}) collective-permute-start(bf16[4,160,128]{2,1,0:T(8,128)(2,1)S(1)} %get-tuple-element.25.refs_7_), channel_id=1, source_target_pairs={{1,10},{3,12},{5,14},{2,9},{4,11},{6,13}} | collective-permute-start | bytes 491528 | tf_op jit(solution)/shard_map/ppermute | solution.py:365
  18.9 0.7 collective-permute-start.5
  26.5 1.4 %collective-permute-start.9 = (bf16[4,160,128]{2,1,0:T(8,128)(2,1)S(1)}, bf16[4,160,128]{2,1,0:T(8,128)(2,1)S(1)}, u32[]{:S(2)}, u32[]{:S(2)}) collective-permute-start(bf16[4,160,128]{2,1,0:T(8,128)(2,1)S(1)} %get-tuple-element.31.refs_8_), channel_id=1, source_target_pairs={{8,16},{9,17},{10,18},{11,19},{12,20},{13,21},{14,22},{15,23},{0,8... | collective-permute-start | bytes 491528 | tf_op jit(solution)/shard_map/ppermute | solution.py:365
  27.2 1.4 %collective-permute-start.11 = (bf16[4,160,128]{2,1,0:T(8,128)(2,1)S(1)}, bf16[4,160,128]{2,1,0:T(8,128)(2,1)S(1)}, u32[]{:S(2)}, u32[]{:S(2)}) collective-permute-start(bf16[4,160,128]{2,1,0:T(8,128)(2,1)S(1)} %get-tuple-element.31.refs_8_), channel_id=1, source_target_pairs={{9,18},{11,20},{13,22},{10,17},{12,19},{14,21},{1,10},{3,12},{5,14... | collective-permute-start | bytes 491528 | tf_op jit(solution)/shard_map/ppermute | solution.py:365
  27.9 0.7 collective-permute-start.10
  29.2 36.8 %collective-permute-start.12 = (bf16[4,160,128]{2,1,0:T(8,128)(2,1)S(1)}, bf16[4,160,128]{2,1,0:T(8,128)(2,1)S(1)}, u32[]{:S(2)}, u32[]{:S(2)}) collective-permute-start(bf16[4,160,128]{2,1,0:T(8,128)(2,1)S(1)} %get-tuple-element.33.refs_9_), channel_id=1, source_target_pairs={{16,24},{17,25},{18,26},{19,27},{20,28},{21,29},{22,30},{23,31},{8... | collective-permute-start | bytes 491528 | tf_op jit(solution)/shard_map/ppermute | solution.py:365
  30.5 38.7 %collective-permute-start.14 = (bf16[4,160,128]{2,1,0:T(8,128)(2,1)S(1)}, bf16[4,160,128]{2,1,0:T(8,128)(2,1)S(1)}, u32[]{:S(2)}, u32[]{:S(2)}) collective-permute-start(bf16[4,160,128]{2,1,0:T(8,128)(2,1)S(1)} %get-tuple-element.33.refs_9_), channel_id=1, source_target_pairs={{17,26},{19,28},{21,30},{18,25},{20,27},{22,29},{9,18},{11,20},{13... | collective-permute-start | bytes 491528 | tf_op jit(solution)/shard_map/ppermute | solution.py:365
  65.9 4.3 %collective-permute-start.13 = (bf16[4,160,128]{2,1,0:T(8,128)(2,1)S(1)}, bf16[4,160,128]{2,1,0:T(8,128)(2,1)S(1)}, u32[]{:S(2)}, u32[]{:S(2)}) collective-permute-start(bf16[4,160,128]{2,1,0:T(8,128)(2,1)S(1)} %collective-permute-done.12.refs_0_), channel_id=1, source_target_pairs={{24,25},{25,24},{26,27},{27,26},{28,29},{29,28},{30,31},{31,30},{1... | collective-permute-start | bytes 491528 | tf_op jit(solution)/shard_map/ppermute | solution.py:362
  71.9 10.5 %collective-permute-start.15 = (bf16[4,160,128]{2,1,0:T(8,128)(2,1)S(1)}, bf16[4,160,128]{2,1,0:T(8,128)(2,1)S(1)}, u32[]{:S(2)}, u32[]{:S(2)}) collective-permute-start(bf16[4,160,128]{2,1,0:T(8,128)(2,1)S(1)} %get-tuple-element.35.refs_10_), channel_id=1, source_target_pairs={{16,24},{17,25},{18,26},{19,27},{20,28},{21,29},{22,30},{23,31}} | collective-permute-start | bytes 491528 | tf_op jit(solution)/shard_map/ppermute | solution.py:365
  73.2 12.5 %collective-permute-start.17 = (bf16[4,160,128]{2,1,0:T(8,128)(2,1)S(1)}, bf16[4,160,128]{2,1,0:T(8,128)(2,1)S(1)}, u32[]{:S(2)}, u32[]{:S(2)}) collective-permute-start(bf16[4,160,128]{2,1,0:T(8,128)(2,1)S(1)} %get-tuple-element.35.refs_10_), channel_id=1, source_target_pairs={{17,26},{19,28},{21,30},{18,25},{20,27},{22,29}} | collective-permute-start | bytes 491528 | tf_op jit(solution)/shard_map/ppermute | solution.py:365
  82.4 4.3 %collective-permute-start.16 = (bf16[4,160,128]{2,1,0:T(8,128)(2,1)S(1)}, bf16[4,160,128]{2,1,0:T(8,128)(2,1)S(1)}, u32[]{:S(2)}, u32[]{:S(2)}) collective-permute-start(bf16[4,160,128]{2,1,0:T(8,128)(2,1)S(1)} %collective-permute-done.15.refs_0_), channel_id=1, source_target_pairs={{24,25},{25,24},{26,27},{27,26},{28,29},{29,28},{30,31},{31,30}} | collective-permute-start | bytes 491528 | tf_op jit(solution)/shard_map/ppermute | solution.py:362

commit v2 on v1

--- a/solution.py
+++ b/solution.py
@@ -34,13 +34,6 @@
     for i in range(lines.shape[0]):
         lines[i, 0:PAD] = edge
         lines[i, lines.shape[1] - PAD :] = edge
-
-
-def rows_dot(s_ref, first, count, w, layer, times):
-    width, depth = s_ref.shape[1:]
-    taps = jnp.concatenate([s_ref[pl.ds(first + i, count)].reshape(count * width, depth) for i in range(3)], axis=1)
-    weights = jnp.concatenate([jnp.concatenate([w[layer, k, t] for t in times], axis=1) for k in range(9)], axis=0)
-    return jnp.dot(taps, weights, preferred_element_type=F32)
 
 
 def pairs_dot(first, count, w, layer, *terms):
@@ -137,6 +130,10 @@
         messages(inner, cross)
 
 
+def level_rows(rows, layers, level):
+    return rows - layers + 1 + level, rows + 2 * (layers - 1 - level)
+
+
 def pieces(count):
     parts, at = [], 0
     while at < count:
@@ -161,8 +158,8 @@
     behind = take(1)[0] if one else None
     results = take(segments) if not zero else []
     out = take(1)[0]
-    ahead = take(1)[0] if zero else None
-    x, s, lines, part, sems = refs
+    kept = take(1)[0] if zero else None
+    x, scratch, lines, part, sems = refs
     rows, width, channels = out.shape[-3:]
     layers = w.shape[0]
     starts = message_starts(layers)
@@ -205,7 +202,7 @@
 
         clear_lines(lines)
 
-        def build(row, line):
+        def build(s, row, line):
             half = x[row].astype(F32) * 0.5
             inside = jnp.logical_and(row >= low, row < high).astype(F32)
             taps_into(s, row, (half + half * jnp.tanh(half)) * inside, line)
@@ -215,25 +212,21 @@
             @pl.when(level >= begin)
             def _(level=level):
                 layer = level - begin
-                first = rows - layers + 1 + level
-                count = rows + 2 * (layers - 1 - level)
+                first, count = level_rows(rows, layers, level)
+                s = kept.at[level] if frame == 0 else scratch
 
                 def two(i, _):
-                    build(first - 1 + 2 * i, lines.at[0])
-                    build(first + 2 * i, lines.at[1])
+                    build(s, first - 1 + 2 * i, lines.at[0])
+                    build(s, first + 2 * i, lines.at[1])
                     return 0
 
                 lax.fori_loop(0, count // 2 + 1, two, 0)
                 offset = bias[pl.ds(layer, 1), :].reshape(1, 1, channels)
-                for start, step in [(0, count)] if frame == 0 else pieces(count):
+                for start, step in pieces(count):
                     at = first + start
+                    mine = pairs_dot(at - 1, step // 2, w, layer, (s, 2))
                     known = part[level, at : at + step].astype(F32) + offset
-                    if frame == 0:
-                        total = rows_dot(s, at - 1, step, w, layer, (2, 1))
-                        mine = total[:, :channels].reshape(step, width, channels)
-                        ahead[level, at : at + step] = total[:, channels:].reshape(step, width, channels).astype(BF16)
-                    else:
-                        mine = pairs_dot(at - 1, step // 2, w, layer, (s, 2))
+                    if frame == 1:
                         known = known + behind[level, at : at + step].astype(F32)
                     x[at : at + step] = (x[at : at + step].astype(F32) + (mine + known)).astype(BF16)
 
@@ -271,6 +264,24 @@
         def _(section=section):
             for copy in finished(section):
                 copy.wait()
+
+
+def ahead_kernel(tick, flags, w, kept, ahead):
+    layers, rows = kept.shape[0], kept.shape[1] // 3
+    begin = layers - flags[2]
+
+    @pl.when(flags[0] == tick)
+    def _():
+        for level in range(layers):
+
+            @pl.when(level >= begin)
+            def _(level=level):
+                first, count = level_rows(rows, layers, level)
+                for start, step in pieces(count):
+                    at = first + start
+                    ahead[level, at : at + step] = pairs_dot(
+                        at - 1, step // 2, w, level - begin, (kept.at[level], 1)
+                    ).astype(BF16)
 
 
 def in_vmem(count):
@@ -323,7 +334,7 @@
     extra = (list(clip) if tick < 2 else []) + (list(received) if one else [])
     extra += (list(sums0) if zero else []) + (list(sums1) + [behind] if one else [])
     if zero:
-        outs = [jax.ShapeDtypeStruct((rows, width, channels), BF16), jax.ShapeDtypeStruct(every, BF16)]
+        outs = [jax.ShapeDtypeStruct((rows, width, channels), BF16), jax.ShapeDtypeStruct(every[:3] + (3 * channels,), BF16)]
         specs = in_vmem(2)
     else:
         extra += results
@@ -342,10 +353,25 @@
         ],
         compiler_params=pltpu.CompilerParams(vmem_limit_bytes=LIMIT),
         cost_estimate=pl.CostEstimate(
-            flops=pixels * 18 * 2 * channels * channels, bytes_accessed=4000000, transcendentals=pixels * channels
+            flops=pixels * 9 * 2 * channels * channels, bytes_accessed=4000000, transcendentals=pixels * channels
         ),
         name="tick",
     )(flags, weights, biases, *extra)
+
+
+def ahead_call(tick, flags, weights, kept):
+    layers, extent, width, depth = kept.shape
+    return pl.pallas_call(
+        functools.partial(ahead_kernel, tick),
+        out_shape=jax.ShapeDtypeStruct((layers, extent, width, depth // 3), BF16),
+        in_specs=[in_smem()] + in_vmem(2),
+        out_specs=in_vmem(1)[0],
+        compiler_params=pltpu.CompilerParams(vmem_limit_bytes=LIMIT),
+        cost_estimate=pl.CostEstimate(
+            flops=layers * extent * width * 6 * depth * depth // 3, bytes_accessed=4000000, transcendentals=0
+        ),
+        name="ahead",
+    )(flags, weights, kept)
 
 
 def per_device(clip, caches, weights, biases, section_layers):
@@ -384,10 +410,11 @@
             tick, segments, bands, flags, halves, received, weights, biases, sums0, sums1, behind, results
         )
         if tick < segments:
-            (behind,) = later
+            behind = ahead_call(tick, flags, weights, later[0])
             results.append(x)
             sources = [s for s in (tick, tick - 1) if 0 <= s < segments - 1]
             own, cross = ahead(x, straight, sources), ahead(x, between, sources)
+            own, behind = lax.optimization_barrier((own, behind))
             received = (own, swap(own, in_chip, [s + 1 for s in sources]), cross)
     return x[None]
 

time: 88 us -> 89.8 us (1.020)
  Pallas kernels: 9.98 us -> 16.4 us
  waiting for transfers between devices: 54.2 us -> 49.9 us
    pallas_call x0 -> x4, Pallas kernels: none -> 3.19 us  [ahead_call(): pl.pallas_call(functools.partial(ahead_kernel, tick), out_shape=jax.Shape...]
    ppermute x8, waiting for transfers between devices: 42.1 us -> 38.9 us  [ahead(): lax.ppermute(value, axes, [(s * bands + a, (s + 1) * bands + b) for s in...]
    pallas_call x2, Pallas kernels: 4.4 us -> 6.19 us  [history_call(): pl.pallas_call(functools.partial(history_kernel, frame), out_shape=tuple(...]
    pallas_call x5, Pallas kernels: 5.58 us -> 6.99 us  [tick_call(): pl.pallas_call(functools.partial(tick_kernel, tick, segments, bands), out...]
    ppermute x9, waiting for transfers between devices: 12.1 us -> 10.9 us  [swap(): lax.ppermute(value, axes, [(s * bands + a, s * bands + b) for s in chosen...]
  transfers between devices with their start and end apart: 18 -> 18, of which waited for: 6 -> 6; matrix products, arithmetic and copies ran while one was open for 0% -> 0% of each run, Pallas kernels for 6% -> 11%
where the time goes in v2:
time: 89.8 us; the launch traced here: 91.4 us
  waiting for transfers between devices  49.9 us (56%)
  starting transfers between devices  23.9 us (27%)
  Pallas kernels  16.4 us (18%)
  between operations  1.17 us (1%)
    ppermute x8, waiting for transfers between devices, ahead(): lax.ppermute(value, axes, [(s * bands + a, (s + 1) * bands + b) for s in...  38.9 us
    ppermute x9, starting transfers between devices, swap(): lax.ppermute(value, axes, [(s * bands + a, s * bands + b) for s in chosen...  15.2 us
    ppermute x9, waiting for transfers between devices, swap(): lax.ppermute(value, axes, [(s * bands + a, s * bands + b) for s in chosen...  10.9 us
    ppermute x8, starting transfers between devices, ahead(): lax.ppermute(value, axes, [(s * bands + a, (s + 1) * bands + b) for s in...  8.03 us
    pallas_call x5, Pallas kernels, tick_call(): pl.pallas_call(functools.partial(tick_kernel, tick, segments, bands), out...  6.99 us
    pallas_call x2, Pallas kernels, history_call(): pl.pallas_call(functools.partial(history_kernel, frame), out_shape=tuple(...  6.19 us
    pallas_call x4, Pallas kernels, ahead_call(): pl.pallas_call(functools.partial(ahead_kernel, tick), out_shape=jax.Shape...  3.19 us
  transfers between devices with their start and end apart: 18, of which 6 were waited for; matrix products, arithmetic and copies ran while one was open for 0% of the time, Pallas kernels for 11%

profile of v2, /device:TPU:29, one launch (start us, length us, event | category | flops | bytes accessed | tf_op | source)
XLA Modules:
  0.0 91.4 jit_solution(3119361830661918869)
XLA Ops:
  0.0 0.7 collective-permute-start.1
  1.4 4.2 %history.2 = (bf16[4,6,160,128]{3,2,1,0:T(8,128)(2,1)S(1)}, bf16[10,160,128]{2,1,0:T(8,128)(2,1)S(1)}, bf16[10,160,128]{2,1,0:T(8,128)(2,1)S(1)}) custom-call(s32[3]{0:T(128)S(1)} %pad_add_fusion.flags, bf16[4,2,4,160,128]{4,3,2,1,0:T(8,128)(2,1)} %bitcast.17, bf16[4,9,3,128,128]{4,3,2,1,0:T(8,128)(2,1)} %bitcast.6), custom_call_target="tpu_custom_call" | custom-call | flops 2264924160 | bytes 4000000 | tf_op jit(solution)/shard_map/history/pallas_call | solution.py:314
  5.6 0.7 collective-permute-start.2
  6.4 3.0 %collective-permute-start.3 = (bf16[10,160,128]{2,1,0:T(8,128)(2,1)S(1)}, bf16[10,160,128]{2,1,0:T(8,128)(2,1)S(1)}, u32[]{:S(2)}, u32[]{:S(2)}) collective-permute-start(bf16[10,160,128]{2,1,0:T(8,128)(2,1)S(1)} %get-tuple-element.32), channel_id=1, source_target_pairs={{1,2},{3,4},{5,6},{2,1},{4,3},{6,5},{9,10},{11,12},{13,14},{10,9},... | collective-permute-start | bytes 1228808 | tf_op jit(solution)/shard_map/ppermute | solution.py:388
  9.4 0.7 collective-permute-start
  10.1 2.0 %history.3 = (bf16[4,6,160,128]{3,2,1,0:T(8,128)(2,1)S(1)}, bf16[10,160,128]{2,1,0:T(8,128)(2,1)S(1)}, bf16[10,160,128]{2,1,0:T(8,128)(2,1)S(1)}) custom-call(s32[3]{0:T(128)S(1)} %pad_add_fusion.flags, bf16[4,2,4,160,128]{4,3,2,1,0:T(8,128)(2,1)S(1)} %bitcast.18, bf16[4,9,3,128,128]{4,3,2,1,0:T(8,128)(2,1)S(1)} %bitcast.7), custom_call_target="tpu_custom_call" | custom-call | flops 1132462080 | bytes 4000000 | tf_op jit(solution)/shard_map/history/pallas_call | solution.py:314
  12.6 2.1 %collective-permute-start.8 = (bf16[10,160,128]{2,1,0:T(8,128)(2,1)S(1)}, bf16[10,160,128]{2,1,0:T(8,128)(2,1)S(1)}, u32[]{:S(2)}, u32[]{:S(2)}) collective-permute-start(bf16[10,160,128]{2,1,0:T(8,128)(2,1)S(1)} %get-tuple-element.39), channel_id=1, source_target_pairs={{1,2},{3,4},{5,6},{2,1},{4,3},{6,5},{9,10},{11,12},{13,14},{10,9},... | collective-permute-start | bytes 1228808 | tf_op jit(solution)/shard_map/ppermute | solution.py:388
  14.8 3.3 %collective-permute-done.3.refs_5_.refs_8_ = bf16[10,160,128]{2,1,0:T(8,128)(2,1)S(1)} collective-permute-done((bf16[10,160,128]{2,1,0:T(8,128)(2,1)S(1)}, bf16[10,160,128]{2,1,0:T(8,128)(2,1)S(1)}, u32[]{:S(2)}, u32[]{:S(2)}) %collective-permute-start.3) | collective-permute-done | bytes 409632 | tf_op jit(solution)/shard_map/ppermute | solution.py:388
  18.1 0.6 tick.5
  18.7 0.7 collective-permute-start.6
  19.4 0.7 collective-permute-start.4
  20.0 0.6 ahead.4.refs_12_
  20.6 0.7 collective-permute-start.5
  21.3 5.6 %collective-permute-done.8.refs_11_.refs_8_.refs_5_ = bf16[10,160,128]{2,1,0:T(8,128)(2,1)S(1)} collective-permute-done((bf16[10,160,128]{2,1,0:T(8,128)(2,1)S(1)}, bf16[10,160,128]{2,1,0:T(8,128)(2,1)S(1)}, u32[]{:S(2)}, u32[]{:S(2)}) %collective-permute-start.8) | collective-permute-done | bytes 409632 | tf_op jit(solution)/shard_map/ppermute | solution.py:388
  26.9 0.6 tick.6
  27.5 0.7 collective-permute-start.11
  28.2 0.9 collective-permute-start.9
  29.6 0.7 collective-permute-start.10
  30.3 0.6 tick.7
  30.9 1.3 %collective-permute-start.14 = (bf16[4,160,128]{2,1,0:T(8,128)(2,1)S(1)}, bf16[4,160,128]{2,1,0:T(8,128)(2,1)S(1)}, u32[]{:S(2)}, u32[]{:S(2)}) collective-permute-start(bf16[4,160,128]{2,1,0:T(8,128)(2,1)S(1)} %get-tuple-element.45.refs_9_), channel_id=1, source_target_pairs={{17,26},{19,28},{21,30},{18,25},{20,27},{22,29},{9,18},{11,20},{13... | collective-permute-start | bytes 491528 | tf_op jit(solution)/shard_map/ppermute | solution.py:391
  32.2 1.3 %collective-permute-start.12 = (bf16[4,160,128]{2,1,0:T(8,128)(2,1)S(1)}, bf16[4,160,128]{2,1,0:T(8,128)(2,1)S(1)}, u32[]{:S(2)}, u32[]{:S(2)}) collective-permute-start(bf16[4,160,128]{2,1,0:T(8,128)(2,1)S(1)} %get-tuple-element.45.refs_9_), channel_id=1, source_target_pairs={{16,24},{17,25},{18,26},{19,27},{20,28},{21,29},{22,30},{23,31},{8... | collective-permute-start | bytes 491528 | tf_op jit(solution)/shard_map/ppermute | solution.py:391
  34.0 33.7 %collective-permute-done.12.refs_0_ = bf16[4,160,128]{2,1,0:T(8,128)(2,1)S(1)} collective-permute-done((bf16[4,160,128]{2,1,0:T(8,128)(2,1)S(1)}, bf16[4,160,128]{2,1,0:T(8,128)(2,1)S(1)}, u32[]{:S(2)}, u32[]{:S(2)}) %collective-permute-start.12) | collective-permute-done | bytes 163872 | tf_op jit(solution)/shard_map/ppermute | solution.py:391
  67.7 2.8 %collective-permute-start.13 = (bf16[4,160,128]{2,1,0:T(8,128)(2,1)S(1)}, bf16[4,160,128]{2,1,0:T(8,128)(2,1)S(1)}, u32[]{:S(2)}, u32[]{:S(2)}) collective-permute-start(bf16[4,160,128]{2,1,0:T(8,128)(2,1)S(1)} %collective-permute-done.12.refs_0_), channel_id=1, source_target_pairs={{24,25},{25,24},{26,27},{27,26},{28,29},{29,28},{30,31},{31,30},{1... | collective-permute-start | bytes 491528 | tf_op jit(solution)/shard_map/ppermute | solution.py:388
  70.5 1.0 %collective-permute-done.13.refs_1_ = bf16[4,160,128]{2,1,0:T(8,128)(2,1)S(1)} collective-permute-done((bf16[4,160,128]{2,1,0:T(8,128)(2,1)S(1)}, bf16[4,160,128]{2,1,0:T(8,128)(2,1)S(1)}, u32[]{:S(2)}, u32[]{:S(2)}) %collective-permute-start.13) | collective-permute-done | bytes 163872 | tf_op jit(solution)/shard_map/ppermute | solution.py:388
  71.5 2.4 %tick.8 = (bf16[4,160,128]{2,1,0:T(8,128)(2,1)S(1)}, bf16[4,12,160,384]{3,2,1,0:T(8,128)(2,1)S(1)}) custom-call(s32[3]{0:T(128)S(1)} %pad_add_fusion.flags, bf16[4,9,3,128,128]{4,3,2,1,0:T(8,128)(2,1)S(1)} %bitcast.14, f32[4,128]{1,0:T(4,128)S(1)} %bitcast.22, bf16[4,160,128]{2,1,0:T(8,128)(2,1)S(1)} %collective-permute-done.12.refs_0_, ...), custom_call_target="tpu_custom_call" | custom-call | flops 1321205760 | bytes 4000000 | tf_op jit(solution)/shard_map/tick/pallas_call | solution.py:342
  73.9 1.3 %collective-permute-start.17 = (bf16[4,160,128]{2,1,0:T(8,128)(2,1)S(1)}, bf16[4,160,128]{2,1,0:T(8,128)(2,1)S(1)}, u32[]{:S(2)}, u32[]{:S(2)}) collective-permute-start(bf16[4,160,128]{2,1,0:T(8,128)(2,1)S(1)} %get-tuple-element.49.refs_10_), channel_id=1, source_target_pairs={{17,26},{19,28},{21,30},{18,25},{20,27},{22,29}} | collective-permute-start | bytes 491528 | tf_op jit(solution)/shard_map/ppermute | solution.py:391
  75.2 1.3 %collective-permute-start.15 = (bf16[4,160,128]{2,1,0:T(8,128)(2,1)S(1)}, bf16[4,160,128]{2,1,0:T(8,128)(2,1)S(1)}, u32[]{:S(2)}, u32[]{:S(2)}) collective-permute-start(bf16[4,160,128]{2,1,0:T(8,128)(2,1)S(1)} %get-tuple-element.49.refs_10_), channel_id=1, source_target_pairs={{16,24},{17,25},{18,26},{19,27},{20,28},{21,29},{22,30},{23,31}} | collective-permute-start | bytes 491528 | tf_op jit(solution)/shard_map/ppermute | solution.py:391
  76.5 1.5 %ahead.7.refs_6_ = bf16[4,12,160,128]{3,2,1,0:T(8,128)(2,1)S(1)} custom-call(s32[3]{0:T(128)S(1)} %pad_add_fusion.flags, bf16[4,9,3,128,128]{4,3,2,1,0:T(8,128)(2,1)S(1)} %bitcast.15, bf16[4,12,160,384]{3,2,1,0:T(8,128)(2,1)S(1)} %get-tuple-element.50.kept), custom_call_target="tpu_custom_call" | custom-call | flops 2264924160 | bytes 4000000 | tf_op jit(solution)/shard_map/ahead/pallas_call | solution.py:364
  78.1 5.3 %collective-permute-done.15.refs_0_ = bf16[4,160,128]{2,1,0:T(8,128)(2,1)S(1)} collective-permute-done((bf16[4,160,128]{2,1,0:T(8,128)(2,1)S(1)}, bf16[4,160,128]{2,1,0:T(8,128)(2,1)S(1)}, u32[]{:S(2)}, u32[]{:S(2)}) %collective-permute-start.15) | collective-permute-done | bytes 163872 | tf_op jit(solution)/shard_map/ppermute | solution.py:391
  83.3 4.0 %collective-permute-start.16 = (bf16[4,160,128]{2,1,0:T(8,128)(2,1)S(1)}, bf16[4,160,128]{2,1,0:T(8,128)(2,1)S(1)}, u32[]{:S(2)}, u32[]{:S(2)}) collective-permute-start(bf16[4,160,128]{2,1,0:T(8,128)(2,1)S(1)} %collective-permute-done.15.refs_0_), channel_id=1, source_target_pairs={{24,25},{25,24},{26,27},{27,26},{28,29},{29,28},{30,31},{31,30}} | collective-permute-start | bytes 491528 | tf_op jit(solution)/shard_map/ppermute | solution.py:388
  87.3 1.0 %collective-permute-done.16.refs_1_ = bf16[4,160,128]{2,1,0:T(8,128)(2,1)S(1)} collective-permute-done((bf16[4,160,128]{2,1,0:T(8,128)(2,1)S(1)}, bf16[4,160,128]{2,1,0:T(8,128)(2,1)S(1)}, u32[]{:S(2)}, u32[]{:S(2)}) %collective-permute-start.16) | collective-permute-done | bytes 163872 | tf_op jit(solution)/shard_map/ppermute | solution.py:388
  88.3 2.9 %tick.9 = bf16[2,4,160,128]{3,2,1,0:T(8,128)(2,1)} custom-call(s32[3]{0:T(128)S(1)} %pad_add_fusion.flags, bf16[4,9,3,128,128]{4,3,2,1,0:T(8,128)(2,1)S(1)} %bitcast.16, f32[4,128]{1,0:T(4,128)S(1)} %bitcast.23, bf16[4,160,128]{2,1,0:T(8,128)(2,1)S(1)} %collective-permute-done.15.refs_0_, bf16[4,160,128]{2,1,0:T(8,128)(2,1)S(1)} %collective-permute-done.16.refs_1_, ...), custom_call_target="tpu_custom_call" | custom-call | flops 1321205760 | bytes 4000000 | tf_op jit(solution)/shard_map/tick/pallas_call | solution.py:342
  (24 shorter events, 1.7 us)
Async XLA Ops:
  0.0 10.1 %collective-permute-start.1 = (bf16[2,4,160,128]{3,2,1,0:T(8,128)(2,1)}, bf16[2,4,160,128]{3,2,1,0:T(8,128)(2,1)S(1)}, u32[]{:S(2)}, u32[]{:S(2)}) collective-permute-start(bf16[2,4,160,128]{3,2,1,0:T(8,128)(2,1)} %refs_0_.3), channel_id=1, source_target_pairs={{9,2},{11,4},{13,6},{10,1},{12,3},{14,5}} | collective-permute-start | bytes 983048 | tf_op jit(solution)/shard_map/ppermute | solution.py:395
  1.4 8.0 %copy-start.1 = (bf16[2,4,160,128]{3,2,1,0:T(8,128)(2,1)S(1)}, bf16[2,4,160,128]{3,2,1,0:T(8,128)(2,1)}, u32[]{:S(2)}) copy-start(bf16[2,4,160,128]{3,2,1,0:T(8,128)(2,1)} %refs_0_.3) | copy-start | bytes 983044
  1.4 8.7 %copy-start = (bf16[1,4,9,3,128,128]{5,4,3,2,1,0:T(8,128)(2,1)S(1)}, bf16[1,4,9,3,128,128]{5,4,3,2,1,0:T(8,128)(2,1)}, u32[]{:S(2)}) copy-start(bf16[1,4,9,3,128,128]{5,4,3,2,1,0:T(8,128)(2,1)} %param.7) | copy-start | bytes 10616836
  1.4 8.7 %copy-start.2 = (bf16[1,4,2,4,160,128]{5,4,3,2,1,0:T(8,128)(2,1)S(1)}, bf16[1,4,2,4,160,128]{5,4,3,2,1,0:T(8,128)(2,1)}, u32[]{:S(2)}) copy-start(bf16[1,4,2,4,160,128]{5,4,3,2,1,0:T(8,128)(2,1)} %param.6) | copy-start | bytes 3932164
  5.6 12.5 %copy-start.3 = (f32[1,4,128]{2,1,0:T(4,128)S(1)}, f32[1,4,128]{2,1,0:T(4,128)}, u32[]{:S(2)}) copy-start(f32[1,4,128]{2,1,0:T(4,128)} %param.8) | copy-start | bytes 6148
  5.6 9.1 %collective-permute-start.2 = (bf16[10,160,128]{2,1,0:T(8,128)(2,1)S(1)}, bf16[10,160,128]{2,1,0:T(8,128)(2,1)S(1)}, u32[]{:S(2)}, u32[]{:S(2)}) collective-permute-start(bf16[10,160,128]{2,1,0:T(8,128)(2,1)S(1)} %get-tuple-element.31), channel_id=1, source_target_pairs={{0,1},{1,0},{2,3},{3,2},{4,5},{5,4},{6,7},{7,6},{8,9},{9,8},{10,11... | collective-permute-start | bytes 1228808 | tf_op jit(solution)/shard_map/ppermute | solution.py:388
  6.4 11.7 %collective-permute-start.3 = (bf16[10,160,128]{2,1,0:T(8,128)(2,1)S(1)}, bf16[10,160,128]{2,1,0:T(8,128)(2,1)S(1)}, u32[]{:S(2)}, u32[]{:S(2)}) collective-permute-start(bf16[10,160,128]{2,1,0:T(8,128)(2,1)S(1)} %get-tuple-element.32), channel_id=1, source_target_pairs={{1,2},{3,4},{5,6},{2,1},{4,3},{6,5},{9,10},{11,12},{13,14},{10,9},... | collective-permute-start | bytes 1228808 | tf_op jit(solution)/shard_map/ppermute | solution.py:388
  9.4 5.3 %collective-permute-start = (bf16[2,4,160,128]{3,2,1,0:T(8,128)(2,1)S(1)}, bf16[2,4,160,128]{3,2,1,0:T(8,128)(2,1)S(1)}, u32[]{:S(2)}, u32[]{:S(2)}) collective-permute-start(bf16[2,4,160,128]{3,2,1,0:T(8,128)(2,1)S(1)} %copy-done.1), channel_id=1, source_target_pairs={{0,1},{1,0},{2,3},{3,2},{4,5},{5,4},{6,7},{7,6}} | collective-permute-start | bytes 983048 | tf_op jit(solution)/shard_map/ppermute | solution.py:388
  12.1 9.2 %collective-permute-start.7 = (bf16[10,160,128]{2,1,0:T(8,128)(2,1)S(1)}, bf16[10,160,128]{2,1,0:T(8,128)(2,1)S(1)}, u32[]{:S(2)}, u32[]{:S(2)}) collective-permute-start(bf16[10,160,128]{2,1,0:T(8,128)(2,1)S(1)} %get-tuple-element.38), channel_id=1, source_target_pairs={{0,1},{1,0},{2,3},{3,2},{4,5},{5,4},{6,7},{7,6},{8,9},{9,8},{10,11... | collective-permute-start | bytes 1228808 | tf_op jit(solution)/shard_map/ppermute | solution.py:388
  12.6 14.3 %collective-permute-start.8 = (bf16[10,160,128]{2,1,0:T(8,128)(2,1)S(1)}, bf16[10,160,128]{2,1,0:T(8,128)(2,1)S(1)}, u32[]{:S(2)}, u32[]{:S(2)}) collective-permute-start(bf16[10,160,128]{2,1,0:T(8,128)(2,1)S(1)} %get-tuple-element.39), channel_id=1, source_target_pairs={{1,2},{3,4},{5,6},{2,1},{4,3},{6,5},{9,10},{11,12},{13,14},{10,9},... | collective-permute-start | bytes 1228808 | tf_op jit(solution)/shard_map/ppermute | solution.py:388
  18.7 2.6 %collective-permute-start.6 = (bf16[4,160,128]{2,1,0:T(8,128)(2,1)S(1)}, bf16[4,160,128]{2,1,0:T(8,128)(2,1)S(1)}, u32[]{:S(2)}, u32[]{:S(2)}) collective-permute-start(bf16[4,160,128]{2,1,0:T(8,128)(2,1)S(1)} %get-tuple-element.33.refs_7_), channel_id=1, source_target_pairs={{1,10},{3,12},{5,14},{2,9},{4,11},{6,13}} | collective-permute-start | bytes 491528 | tf_op jit(solution)/shard_map/ppermute | solution.py:391
  19.4 1.2 %collective-permute-start.4 = (bf16[4,160,128]{2,1,0:T(8,128)(2,1)S(1)}, bf16[4,160,128]{2,1,0:T(8,128)(2,1)S(1)}, u32[]{:S(2)}, u32[]{:S(2)}) collective-permute-start(bf16[4,160,128]{2,1,0:T(8,128)(2,1)S(1)} %get-tuple-element.33.refs_7_), channel_id=1, source_target_pairs={{0,8},{1,9},{2,10},{3,11},{4,12},{5,13},{6,14},{7,15}} | collective-permute-start | bytes 491528 | tf_op jit(solution)/shard_map/ppermute | solution.py:391
  20.6 0.7 collective-permute-start.5
  27.5 2.8 %collective-permute-start.11 = (bf16[4,160,128]{2,1,0:T(8,128)(2,1)S(1)}, bf16[4,160,128]{2,1,0:T(8,128)(2,1)S(1)}, u32[]{:S(2)}, u32[]{:S(2)}) collective-permute-start(bf16[4,160,128]{2,1,0:T(8,128)(2,1)S(1)} %get-tuple-element.41.refs_8_), channel_id=1, source_target_pairs={{9,18},{11,20},{13,22},{10,17},{12,19},{14,21},{1,10},{3,12},{5,14... | collective-permute-start | bytes 491528 | tf_op jit(solution)/shard_map/ppermute | solution.py:391
  28.2 1.4 %collective-permute-start.9 = (bf16[4,160,128]{2,1,0:T(8,128)(2,1)S(1)}, bf16[4,160,128]{2,1,0:T(8,128)(2,1)S(1)}, u32[]{:S(2)}, u32[]{:S(2)}) collective-permute-start(bf16[4,160,128]{2,1,0:T(8,128)(2,1)S(1)} %get-tuple-element.41.refs_8_), channel_id=1, source_target_pairs={{8,16},{9,17},{10,18},{11,19},{12,20},{13,21},{14,22},{15,23},{0,8... | collective-permute-start | bytes 491528 | tf_op jit(solution)/shard_map/ppermute | solution.py:391
  29.6 0.7 collective-permute-start.10
  30.9 39.6 %collective-permute-start.14 = (bf16[4,160,128]{2,1,0:T(8,128)(2,1)S(1)}, bf16[4,160,128]{2,1,0:T(8,128)(2,1)S(1)}, u32[]{:S(2)}, u32[]{:S(2)}) collective-permute-start(bf16[4,160,128]{2,1,0:T(8,128)(2,1)S(1)} %get-tuple-element.45.refs_9_), channel_id=1, source_target_pairs={{17,26},{19,28},{21,30},{18,25},{20,27},{22,29},{9,18},{11,20},{13... | collective-permute-start | bytes 491528 | tf_op jit(solution)/shard_map/ppermute | solution.py:391
  32.2 35.5 %collective-permute-start.12 = (bf16[4,160,128]{2,1,0:T(8,128)(2,1)S(1)}, bf16[4,160,128]{2,1,0:T(8,128)(2,1)S(1)}, u32[]{:S(2)}, u32[]{:S(2)}) collective-permute-start(bf16[4,160,128]{2,1,0:T(8,128)(2,1)S(1)} %get-tuple-element.45.refs_9_), channel_id=1, source_target_pairs={{16,24},{17,25},{18,26},{19,27},{20,28},{21,29},{22,30},{23,31},{8... | collective-permute-start | bytes 491528 | tf_op jit(solution)/shard_map/ppermute | solution.py:391
  67.7 3.8 %collective-permute-start.13 = (bf16[4,160,128]{2,1,0:T(8,128)(2,1)S(1)}, bf16[4,160,128]{2,1,0:T(8,128)(2,1)S(1)}, u32[]{:S(2)}, u32[]{:S(2)}) collective-permute-start(bf16[4,160,128]{2,1,0:T(8,128)(2,1)S(1)} %collective-permute-done.12.refs_0_), channel_id=1, source_target_pairs={{24,25},{25,24},{26,27},{27,26},{28,29},{29,28},{30,31},{31,30},{1... | collective-permute-start | bytes 491528 | tf_op jit(solution)/shard_map/ppermute | solution.py:388
  73.9 13.4 %collective-permute-start.17 = (bf16[4,160,128]{2,1,0:T(8,128)(2,1)S(1)}, bf16[4,160,128]{2,1,0:T(8,128)(2,1)S(1)}, u32[]{:S(2)}, u32[]{:S(2)}) collective-permute-start(bf16[4,160,128]{2,1,0:T(8,128)(2,1)S(1)} %get-tuple-element.49.refs_10_), channel_id=1, source_target_pairs={{17,26},{19,28},{21,30},{18,25},{20,27},{22,29}} | collective-permute-start | bytes 491528 | tf_op jit(solution)/shard_map/ppermute | solution.py:391
  75.2 8.1 %collective-permute-start.15 = (bf16[4,160,128]{2,1,0:T(8,128)(2,1)S(1)}, bf16[4,160,128]{2,1,0:T(8,128)(2,1)S(1)}, u32[]{:S(2)}, u32[]{:S(2)}) collective-permute-start(bf16[4,160,128]{2,1,0:T(8,128)(2,1)S(1)} %get-tuple-element.49.refs_10_), channel_id=1, source_target_pairs={{16,24},{17,25},{18,26},{19,27},{20,28},{21,29},{22,30},{23,31}} | collective-permute-start | bytes 491528 | tf_op jit(solution)/shard_map/ppermute | solution.py:391
  83.3 5.0 %collective-permute-start.16 = (bf16[4,160,128]{2,1,0:T(8,128)(2,1)S(1)}, bf16[4,160,128]{2,1,0:T(8,128)(2,1)S(1)}, u32[]{:S(2)}, u32[]{:S(2)}) collective-permute-start(bf16[4,160,128]{2,1,0:T(8,128)(2,1)S(1)} %collective-permute-done.15.refs_0_), channel_id=1, source_target_pairs={{24,25},{25,24},{26,27},{27,26},{28,29},{29,28},{30,31},{31,30}} | collective-permute-start | bytes 491528 | tf_op jit(solution)/shard_map/ppermute | solution.py:388

commit v3 on v2

--- a/solution.py
+++ b/solution.py
@@ -368,7 +368,7 @@
         out_specs=in_vmem(1)[0],
         compiler_params=pltpu.CompilerParams(vmem_limit_bytes=LIMIT),
         cost_estimate=pl.CostEstimate(
-            flops=layers * extent * width * 6 * depth * depth // 3, bytes_accessed=4000000, transcendentals=0
+            flops=1000000, bytes_accessed=1000000, transcendentals=0
         ),
         name="ahead",
     )(flags, weights, kept)

time: 89.8 us -> 86.5 us (0.963)
  waiting for transfers between devices: 49.9 us -> 35 us
  Pallas kernels: 16.4 us -> 26.3 us
  starting transfers between devices: 23.9 us -> 25.7 us
    ppermute x8, waiting for transfers between devices: 38.9 us -> 25.4 us  [ahead(): lax.ppermute(value, axes, [(s * bands + a, (s + 1) * bands + b) for s in...]
    pallas_call x5, Pallas kernels: 6.99 us -> 11.9 us  [tick_call(): pl.pallas_call(functools.partial(tick_kernel, tick, segments, bands), out...]
    pallas_call x2, Pallas kernels: 6.19 us -> 9.79 us  [history_call(): pl.pallas_call(functools.partial(history_kernel, frame), out_shape=tuple(...]
    ppermute x9, starting transfers between devices: 15.2 us -> 17 us  [swap(): lax.ppermute(value, axes, [(s * bands + a, s * bands + b) for s in chosen...]
    pallas_call x4, Pallas kernels: 3.19 us -> 4.67 us  [ahead_call(): pl.pallas_call(functools.partial(ahead_kernel, tick), out_shape=jax.Shape...]
    ppermute x9, waiting for transfers between devices: 10.9 us -> 9.6 us  [swap(): lax.ppermute(value, axes, [(s * bands + a, s * bands + b) for s in chosen...]
  transfers between devices with their start and end apart: 18 -> 18, of which waited for: 6 -> 6; matrix products, arithmetic and copies ran while one was open for 0% -> 0% of each run, Pallas kernels for 11% -> 17%
where the time goes in v3:
time: 86.5 us; the launch traced here: 88.2 us
  waiting for transfers between devices  35 us (40%)
  Pallas kernels  26.3 us (30%)
  starting transfers between devices  25.7 us (30%)
  between operations  1.17 us (1%)
    ppermute x8, waiting for transfers between devices, ahead(): lax.ppermute(value, axes, [(s * bands + a, (s + 1) * bands + b) for s in...  25.4 us
    ppermute x9, starting transfers between devices, swap(): lax.ppermute(value, axes, [(s * bands + a, s * bands + b) for s in chosen...  17 us
    pallas_call x5, Pallas kernels, tick_call(): pl.pallas_call(functools.partial(tick_kernel, tick, segments, bands), out...  11.9 us
    pallas_call x2, Pallas kernels, history_call(): pl.pallas_call(functools.partial(history_kernel, frame), out_shape=tuple(...  9.79 us
    ppermute x9, waiting for transfers between devices, swap(): lax.ppermute(value, axes, [(s * bands + a, s * bands + b) for s in chosen...  9.6 us
    ppermute x8, starting transfers between devices, ahead(): lax.ppermute(value, axes, [(s * bands + a, (s + 1) * bands + b) for s in...  8.03 us
    pallas_call x4, Pallas kernels, ahead_call(): pl.pallas_call(functools.partial(ahead_kernel, tick), out_shape=jax.Shape...  4.67 us
  transfers between devices with their start and end apart: 18, of which 6 were waited for; matrix products, arithmetic and copies ran while one was open for 0% of the time, Pallas kernels for 17%

profile of v3, /device:TPU:29, one launch (start us, length us, event | category | flops | bytes accessed | tf_op | source)
XLA Modules:
  0.0 88.2 jit_solution(1494591504609443563)
XLA Ops:
  0.0 0.7 collective-permute-start.1
  1.4 6.5 %history.2 = (bf16[4,6,160,128]{3,2,1,0:T(8,128)(2,1)S(1)}, bf16[10,160,128]{2,1,0:T(8,128)(2,1)S(1)}, bf16[10,160,128]{2,1,0:T(8,128)(2,1)S(1)}) custom-call(s32[3]{0:T(128)S(1)} %pad_add_fusion.flags, bf16[4,2,4,160,128]{4,3,2,1,0:T(8,128)(2,1)} %bitcast.17, bf16[4,9,3,128,128]{4,3,2,1,0:T(8,128)(2,1)} %bitcast.6), custom_call_target="tpu_custom_call" | custom-call | flops 2264924160 | bytes 4000000 | tf_op jit(solution)/shard_map/history/pallas_call | solution.py:314
  7.9 0.7 collective-permute-start.2
  8.6 3.0 %collective-permute-start.3 = (bf16[10,160,128]{2,1,0:T(8,128)(2,1)S(1)}, bf16[10,160,128]{2,1,0:T(8,128)(2,1)S(1)}, u32[]{:S(2)}, u32[]{:S(2)}) collective-permute-start(bf16[10,160,128]{2,1,0:T(8,128)(2,1)S(1)} %get-tuple-element.32), channel_id=1, source_target_pairs={{1,2},{3,4},{5,6},{2,1},{4,3},{6,5},{9,10},{11,12},{13,14},{10,9},... | collective-permute-start | bytes 1228808 | tf_op jit(solution)/shard_map/ppermute | solution.py:388
  11.7 0.7 collective-permute-start
  12.4 3.3 %history.3 = (bf16[4,6,160,128]{3,2,1,0:T(8,128)(2,1)S(1)}, bf16[10,160,128]{2,1,0:T(8,128)(2,1)S(1)}, bf16[10,160,128]{2,1,0:T(8,128)(2,1)S(1)}) custom-call(s32[3]{0:T(128)S(1)} %pad_add_fusion.flags, bf16[4,2,4,160,128]{4,3,2,1,0:T(8,128)(2,1)S(1)} %bitcast.18, bf16[4,9,3,128,128]{4,3,2,1,0:T(8,128)(2,1)S(1)} %bitcast.7), custom_call_target="tpu_custom_call" | custom-call | flops 1132462080 | bytes 4000000 | tf_op jit(solution)/shard_map/history/pallas_call | solution.py:314
  16.2 2.1 %collective-permute-start.8 = (bf16[10,160,128]{2,1,0:T(8,128)(2,1)S(1)}, bf16[10,160,128]{2,1,0:T(8,128)(2,1)S(1)}, u32[]{:S(2)}, u32[]{:S(2)}) collective-permute-start(bf16[10,160,128]{2,1,0:T(8,128)(2,1)S(1)} %get-tuple-element.39), channel_id=1, source_target_pairs={{1,2},{3,4},{5,6},{2,1},{4,3},{6,5},{9,10},{11,12},{13,14},{10,9},... | collective-permute-start | bytes 1228808 | tf_op jit(solution)/shard_map/ppermute | solution.py:388
  18.4 2.0 %collective-permute-done.3.refs_5_.refs_8_ = bf16[10,160,128]{2,1,0:T(8,128)(2,1)S(1)} collective-permute-done((bf16[10,160,128]{2,1,0:T(8,128)(2,1)S(1)}, bf16[10,160,128]{2,1,0:T(8,128)(2,1)S(1)}, u32[]{:S(2)}, u32[]{:S(2)}) %collective-permute-start.3) | collective-permute-done | bytes 409632 | tf_op jit(solution)/shard_map/ppermute | solution.py:388
  20.4 0.6 tick.5
  21.0 0.7 collective-permute-start.4
  21.6 0.7 collective-permute-start.6
  22.3 0.6 ahead.4.refs_12_
  22.9 0.7 collective-permute-start.5
  23.6 5.6 %collective-permute-done.8.refs_11_.refs_8_.refs_5_ = bf16[10,160,128]{2,1,0:T(8,128)(2,1)S(1)} collective-permute-done((bf16[10,160,128]{2,1,0:T(8,128)(2,1)S(1)}, bf16[10,160,128]{2,1,0:T(8,128)(2,1)S(1)}, u32[]{:S(2)}, u32[]{:S(2)}) %collective-permute-start.8) | collective-permute-done | bytes 409632 | tf_op jit(solution)/shard_map/ppermute | solution.py:388
  29.2 0.6 tick.6
  29.7 0.7 collective-permute-start.9
  30.4 0.9 collective-permute-start.11
  31.9 0.7 collective-permute-start.10
  32.6 0.6 tick.7
  33.1 1.3 %collective-permute-start.12 = (bf16[4,160,128]{2,1,0:T(8,128)(2,1)S(1)}, bf16[4,160,128]{2,1,0:T(8,128)(2,1)S(1)}, u32[]{:S(2)}, u32[]{:S(2)}) collective-permute-start(bf16[4,160,128]{2,1,0:T(8,128)(2,1)S(1)} %get-tuple-element.45.refs_9_), channel_id=1, source_target_pairs={{16,24},{17,25},{18,26},{19,27},{20,28},{21,29},{22,30},{23,31},{8... | collective-permute-start | bytes 491528 | tf_op jit(solution)/shard_map/ppermute | solution.py:391
  34.4 1.3 %collective-permute-start.14 = (bf16[4,160,128]{2,1,0:T(8,128)(2,1)S(1)}, bf16[4,160,128]{2,1,0:T(8,128)(2,1)S(1)}, u32[]{:S(2)}, u32[]{:S(2)}) collective-permute-start(bf16[4,160,128]{2,1,0:T(8,128)(2,1)S(1)} %get-tuple-element.45.refs_9_), channel_id=1, source_target_pairs={{17,26},{19,28},{21,30},{18,25},{20,27},{22,29},{9,18},{11,20},{13... | collective-permute-start | bytes 491528 | tf_op jit(solution)/shard_map/ppermute | solution.py:391
  36.3 24.4 %collective-permute-done.12.refs_0_ = bf16[4,160,128]{2,1,0:T(8,128)(2,1)S(1)} collective-permute-done((bf16[4,160,128]{2,1,0:T(8,128)(2,1)S(1)}, bf16[4,160,128]{2,1,0:T(8,128)(2,1)S(1)}, u32[]{:S(2)}, u32[]{:S(2)}) %collective-permute-start.12) | collective-permute-done | bytes 163872 | tf_op jit(solution)/shard_map/ppermute | solution.py:391
  60.7 3.3 %collective-permute-start.13 = (bf16[4,160,128]{2,1,0:T(8,128)(2,1)S(1)}, bf16[4,160,128]{2,1,0:T(8,128)(2,1)S(1)}, u32[]{:S(2)}, u32[]{:S(2)}) collective-permute-start(bf16[4,160,128]{2,1,0:T(8,128)(2,1)S(1)} %collective-permute-done.12.refs_0_), channel_id=1, source_target_pairs={{24,25},{25,24},{26,27},{27,26},{28,29},{29,28},{30,31},{31,30},{1... | collective-permute-start | bytes 491528 | tf_op jit(solution)/shard_map/ppermute | solution.py:388
  64.0 1.0 %collective-permute-done.13.refs_1_ = bf16[4,160,128]{2,1,0:T(8,128)(2,1)S(1)} collective-permute-done((bf16[4,160,128]{2,1,0:T(8,128)(2,1)S(1)}, bf16[4,160,128]{2,1,0:T(8,128)(2,1)S(1)}, u32[]{:S(2)}, u32[]{:S(2)}) %collective-permute-start.13) | collective-permute-done | bytes 163872 | tf_op jit(solution)/shard_map/ppermute | solution.py:388
  65.0 4.8 %tick.8 = (bf16[4,160,128]{2,1,0:T(8,128)(2,1)S(1)}, bf16[4,12,160,384]{3,2,1,0:T(8,128)(2,1)S(1)}) custom-call(s32[3]{0:T(128)S(1)} %pad_add_fusion.flags, bf16[4,9,3,128,128]{4,3,2,1,0:T(8,128)(2,1)S(1)} %bitcast.14, f32[4,128]{1,0:T(4,128)S(1)} %bitcast.22, bf16[4,160,128]{2,1,0:T(8,128)(2,1)S(1)} %collective-permute-done.12.refs_0_, ...), custom_call_target="tpu_custom_call" | custom-call | flops 1321205760 | bytes 4000000 | tf_op jit(solution)/shard_map/tick/pallas_call | solution.py:342
  69.8 1.3 %collective-permute-start.15 = (bf16[4,160,128]{2,1,0:T(8,128)(2,1)S(1)}, bf16[4,160,128]{2,1,0:T(8,128)(2,1)S(1)}, u32[]{:S(2)}, u32[]{:S(2)}) collective-permute-start(bf16[4,160,128]{2,1,0:T(8,128)(2,1)S(1)} %get-tuple-element.49.refs_10_), channel_id=1, source_target_pairs={{16,24},{17,25},{18,26},{19,27},{20,28},{21,29},{22,30},{23,31}} | collective-permute-start | bytes 491528 | tf_op jit(solution)/shard_map/ppermute | solution.py:391
  71.1 1.3 %collective-permute-start.17 = (bf16[4,160,128]{2,1,0:T(8,128)(2,1)S(1)}, bf16[4,160,128]{2,1,0:T(8,128)(2,1)S(1)}, u32[]{:S(2)}, u32[]{:S(2)}) collective-permute-start(bf16[4,160,128]{2,1,0:T(8,128)(2,1)S(1)} %get-tuple-element.49.refs_10_), channel_id=1, source_target_pairs={{17,26},{19,28},{21,30},{18,25},{20,27},{22,29}} | collective-permute-start | bytes 491528 | tf_op jit(solution)/shard_map/ppermute | solution.py:391
  72.4 3.0 %ahead.7.refs_6_ = bf16[4,12,160,128]{3,2,1,0:T(8,128)(2,1)S(1)} custom-call(s32[3]{0:T(128)S(1)} %pad_add_fusion.flags, bf16[4,9,3,128,128]{4,3,2,1,0:T(8,128)(2,1)S(1)} %bitcast.15, bf16[4,12,160,384]{3,2,1,0:T(8,128)(2,1)S(1)} %get-tuple-element.50.kept), custom_call_target="tpu_custom_call" | custom-call | flops 1000000 | bytes 1000000 | tf_op jit(solution)/shard_map/ahead/pallas_call | solution.py:364
  75.4 1.0 %collective-permute-done.15.refs_0_ = bf16[4,160,128]{2,1,0:T(8,128)(2,1)S(1)} collective-permute-done((bf16[4,160,128]{2,1,0:T(8,128)(2,1)S(1)}, bf16[4,160,128]{2,1,0:T(8,128)(2,1)S(1)}, u32[]{:S(2)}, u32[]{:S(2)}) %collective-permute-start.15) | collective-permute-done | bytes 163872 | tf_op jit(solution)/shard_map/ppermute | solution.py:391
  76.4 5.3 %collective-permute-start.16 = (bf16[4,160,128]{2,1,0:T(8,128)(2,1)S(1)}, bf16[4,160,128]{2,1,0:T(8,128)(2,1)S(1)}, u32[]{:S(2)}, u32[]{:S(2)}) collective-permute-start(bf16[4,160,128]{2,1,0:T(8,128)(2,1)S(1)} %collective-permute-done.15.refs_0_), channel_id=1, source_target_pairs={{24,25},{25,24},{26,27},{27,26},{28,29},{29,28},{30,31},{31,30}} | collective-permute-start | bytes 491528 | tf_op jit(solution)/shard_map/ppermute | solution.py:388
  81.7 1.0 %collective-permute-done.16.refs_1_ = bf16[4,160,128]{2,1,0:T(8,128)(2,1)S(1)} collective-permute-done((bf16[4,160,128]{2,1,0:T(8,128)(2,1)S(1)}, bf16[4,160,128]{2,1,0:T(8,128)(2,1)S(1)}, u32[]{:S(2)}, u32[]{:S(2)}) %collective-permute-start.16) | collective-permute-done | bytes 163872 | tf_op jit(solution)/shard_map/ppermute | solution.py:388
  82.7 5.3 %tick.9 = bf16[2,4,160,128]{3,2,1,0:T(8,128)(2,1)} custom-call(s32[3]{0:T(128)S(1)} %pad_add_fusion.flags, bf16[4,9,3,128,128]{4,3,2,1,0:T(8,128)(2,1)S(1)} %bitcast.16, f32[4,128]{1,0:T(4,128)S(1)} %bitcast.23, bf16[4,160,128]{2,1,0:T(8,128)(2,1)S(1)} %collective-permute-done.15.refs_0_, bf16[4,160,128]{2,1,0:T(8,128)(2,1)S(1)} %collective-permute-done.16.refs_1_, ...), custom_call_target="tpu_custom_call" | custom-call | flops 1321205760 | bytes 4000000 | tf_op jit(solution)/shard_map/tick/pallas_call | solution.py:342
  (24 shorter events, 1.7 us)
Async XLA Ops:
  0.0 12.4 %collective-permute-start.1 = (bf16[2,4,160,128]{3,2,1,0:T(8,128)(2,1)}, bf16[2,4,160,128]{3,2,1,0:T(8,128)(2,1)S(1)}, u32[]{:S(2)}, u32[]{:S(2)}) collective-permute-start(bf16[2,4,160,128]{3,2,1,0:T(8,128)(2,1)} %refs_0_.3), channel_id=1, source_target_pairs={{9,2},{11,4},{13,6},{10,1},{12,3},{14,5}} | collective-permute-start | bytes 983048 | tf_op jit(solution)/shard_map/ppermute | solution.py:395
  1.4 10.3 %copy-start.1 = (bf16[2,4,160,128]{3,2,1,0:T(8,128)(2,1)S(1)}, bf16[2,4,160,128]{3,2,1,0:T(8,128)(2,1)}, u32[]{:S(2)}) copy-start(bf16[2,4,160,128]{3,2,1,0:T(8,128)(2,1)} %refs_0_.3) | copy-start | bytes 983044
  1.4 11.0 %copy-start = (bf16[1,4,9,3,128,128]{5,4,3,2,1,0:T(8,128)(2,1)S(1)}, bf16[1,4,9,3,128,128]{5,4,3,2,1,0:T(8,128)(2,1)}, u32[]{:S(2)}) copy-start(bf16[1,4,9,3,128,128]{5,4,3,2,1,0:T(8,128)(2,1)} %param.7) | copy-start | bytes 10616836
  1.4 11.0 %copy-start.2 = (bf16[1,4,2,4,160,128]{5,4,3,2,1,0:T(8,128)(2,1)S(1)}, bf16[1,4,2,4,160,128]{5,4,3,2,1,0:T(8,128)(2,1)}, u32[]{:S(2)}) copy-start(bf16[1,4,2,4,160,128]{5,4,3,2,1,0:T(8,128)(2,1)} %param.6) | copy-start | bytes 3932164
  7.9 12.5 %copy-start.3 = (f32[1,4,128]{2,1,0:T(4,128)S(1)}, f32[1,4,128]{2,1,0:T(4,128)}, u32[]{:S(2)}) copy-start(f32[1,4,128]{2,1,0:T(4,128)} %param.8) | copy-start | bytes 6148
  7.9 10.4 %collective-permute-start.2 = (bf16[10,160,128]{2,1,0:T(8,128)(2,1)S(1)}, bf16[10,160,128]{2,1,0:T(8,128)(2,1)S(1)}, u32[]{:S(2)}, u32[]{:S(2)}) collective-permute-start(bf16[10,160,128]{2,1,0:T(8,128)(2,1)S(1)} %get-tuple-element.31), channel_id=1, source_target_pairs={{0,1},{1,0},{2,3},{3,2},{4,5},{5,4},{6,7},{7,6},{8,9},{9,8},{10,11... | collective-permute-start | bytes 1228808 | tf_op jit(solution)/shard_map/ppermute | solution.py:388
  8.6 11.7 %collective-permute-start.3 = (bf16[10,160,128]{2,1,0:T(8,128)(2,1)S(1)}, bf16[10,160,128]{2,1,0:T(8,128)(2,1)S(1)}, u32[]{:S(2)}, u32[]{:S(2)}) collective-permute-start(bf16[10,160,128]{2,1,0:T(8,128)(2,1)S(1)} %get-tuple-element.32), channel_id=1, source_target_pairs={{1,2},{3,4},{5,6},{2,1},{4,3},{6,5},{9,10},{11,12},{13,14},{10,9},... | collective-permute-start | bytes 1228808 | tf_op jit(solution)/shard_map/ppermute | solution.py:388
  11.7 6.7 %collective-permute-start = (bf16[2,4,160,128]{3,2,1,0:T(8,128)(2,1)S(1)}, bf16[2,4,160,128]{3,2,1,0:T(8,128)(2,1)S(1)}, u32[]{:S(2)}, u32[]{:S(2)}) collective-permute-start(bf16[2,4,160,128]{3,2,1,0:T(8,128)(2,1)S(1)} %copy-done.1), channel_id=1, source_target_pairs={{0,1},{1,0},{2,3},{3,2},{4,5},{5,4},{6,7},{7,6}} | collective-permute-start | bytes 983048 | tf_op jit(solution)/shard_map/ppermute | solution.py:388
  15.7 7.9 %collective-permute-start.7 = (bf16[10,160,128]{2,1,0:T(8,128)(2,1)S(1)}, bf16[10,160,128]{2,1,0:T(8,128)(2,1)S(1)}, u32[]{:S(2)}, u32[]{:S(2)}) collective-permute-start(bf16[10,160,128]{2,1,0:T(8,128)(2,1)S(1)} %get-tuple-element.38), channel_id=1, source_target_pairs={{0,1},{1,0},{2,3},{3,2},{4,5},{5,4},{6,7},{7,6},{8,9},{9,8},{10,11... | collective-permute-start | bytes 1228808 | tf_op jit(solution)/shard_map/ppermute | solution.py:388
  16.2 12.9 %collective-permute-start.8 = (bf16[10,160,128]{2,1,0:T(8,128)(2,1)S(1)}, bf16[10,160,128]{2,1,0:T(8,128)(2,1)S(1)}, u32[]{:S(2)}, u32[]{:S(2)}) collective-permute-start(bf16[10,160,128]{2,1,0:T(8,128)(2,1)S(1)} %get-tuple-element.39), channel_id=1, source_target_pairs={{1,2},{3,4},{5,6},{2,1},{4,3},{6,5},{9,10},{11,12},{13,14},{10,9},... | collective-permute-start | bytes 1228808 | tf_op jit(solution)/shard_map/ppermute | solution.py:388
  21.0 1.9 %collective-permute-start.4 = (bf16[4,160,128]{2,1,0:T(8,128)(2,1)S(1)}, bf16[4,160,128]{2,1,0:T(8,128)(2,1)S(1)}, u32[]{:S(2)}, u32[]{:S(2)}) collective-permute-start(bf16[4,160,128]{2,1,0:T(8,128)(2,1)S(1)} %get-tuple-element.33.refs_7_), channel_id=1, source_target_pairs={{0,8},{1,9},{2,10},{3,11},{4,12},{5,13},{6,14},{7,15}} | collective-permute-start | bytes 491528 | tf_op jit(solution)/shard_map/ppermute | solution.py:391
  21.6 1.9 %collective-permute-start.6 = (bf16[4,160,128]{2,1,0:T(8,128)(2,1)S(1)}, bf16[4,160,128]{2,1,0:T(8,128)(2,1)S(1)}, u32[]{:S(2)}, u32[]{:S(2)}) collective-permute-start(bf16[4,160,128]{2,1,0:T(8,128)(2,1)S(1)} %get-tuple-element.33.refs_7_), channel_id=1, source_target_pairs={{1,10},{3,12},{5,14},{2,9},{4,11},{6,13}} | collective-permute-start | bytes 491528 | tf_op jit(solution)/shard_map/ppermute | solution.py:391
  22.9 0.7 collective-permute-start.5
  29.7 2.1 %collective-permute-start.9 = (bf16[4,160,128]{2,1,0:T(8,128)(2,1)S(1)}, bf16[4,160,128]{2,1,0:T(8,128)(2,1)S(1)}, u32[]{:S(2)}, u32[]{:S(2)}) collective-permute-start(bf16[4,160,128]{2,1,0:T(8,128)(2,1)S(1)} %get-tuple-element.41.refs_8_), channel_id=1, source_target_pairs={{8,16},{9,17},{10,18},{11,19},{12,20},{13,21},{14,22},{15,23},{0,8... | collective-permute-start | bytes 491528 | tf_op jit(solution)/shard_map/ppermute | solution.py:391
  30.4 2.1 %collective-permute-start.11 = (bf16[4,160,128]{2,1,0:T(8,128)(2,1)S(1)}, bf16[4,160,128]{2,1,0:T(8,128)(2,1)S(1)}, u32[]{:S(2)}, u32[]{:S(2)}) collective-permute-start(bf16[4,160,128]{2,1,0:T(8,128)(2,1)S(1)} %get-tuple-element.41.refs_8_), channel_id=1, source_target_pairs={{9,18},{11,20},{13,22},{10,17},{12,19},{14,21},{1,10},{3,12},{5,14... | collective-permute-start | bytes 491528 | tf_op jit(solution)/shard_map/ppermute | solution.py:391
  31.9 0.7 collective-permute-start.10
  33.1 27.5 %collective-permute-start.12 = (bf16[4,160,128]{2,1,0:T(8,128)(2,1)S(1)}, bf16[4,160,128]{2,1,0:T(8,128)(2,1)S(1)}, u32[]{:S(2)}, u32[]{:S(2)}) collective-permute-start(bf16[4,160,128]{2,1,0:T(8,128)(2,1)S(1)} %get-tuple-element.45.refs_9_), channel_id=1, source_target_pairs={{16,24},{17,25},{18,26},{19,27},{20,28},{21,29},{22,30},{23,31},{8... | collective-permute-start | bytes 491528 | tf_op jit(solution)/shard_map/ppermute | solution.py:391
  34.4 29.5 %collective-permute-start.14 = (bf16[4,160,128]{2,1,0:T(8,128)(2,1)S(1)}, bf16[4,160,128]{2,1,0:T(8,128)(2,1)S(1)}, u32[]{:S(2)}, u32[]{:S(2)}) collective-permute-start(bf16[4,160,128]{2,1,0:T(8,128)(2,1)S(1)} %get-tuple-element.45.refs_9_), channel_id=1, source_target_pairs={{17,26},{19,28},{21,30},{18,25},{20,27},{22,29},{9,18},{11,20},{13... | collective-permute-start | bytes 491528 | tf_op jit(solution)/shard_map/ppermute | solution.py:391
  60.7 4.3 %collective-permute-start.13 = (bf16[4,160,128]{2,1,0:T(8,128)(2,1)S(1)}, bf16[4,160,128]{2,1,0:T(8,128)(2,1)S(1)}, u32[]{:S(2)}, u32[]{:S(2)}) collective-permute-start(bf16[4,160,128]{2,1,0:T(8,128)(2,1)S(1)} %collective-permute-done.12.refs_0_), channel_id=1, source_target_pairs={{24,25},{25,24},{26,27},{27,26},{28,29},{29,28},{30,31},{31,30},{1... | collective-permute-start | bytes 491528 | tf_op jit(solution)/shard_map/ppermute | solution.py:388
  69.8 6.6 %collective-permute-start.15 = (bf16[4,160,128]{2,1,0:T(8,128)(2,1)S(1)}, bf16[4,160,128]{2,1,0:T(8,128)(2,1)S(1)}, u32[]{:S(2)}, u32[]{:S(2)}) collective-permute-start(bf16[4,160,128]{2,1,0:T(8,128)(2,1)S(1)} %get-tuple-element.49.refs_10_), channel_id=1, source_target_pairs={{16,24},{17,25},{18,26},{19,27},{20,28},{21,29},{22,30},{23,31}} | collective-permute-start | bytes 491528 | tf_op jit(solution)/shard_map/ppermute | solution.py:391
  71.1 10.6 %collective-permute-start.17 = (bf16[4,160,128]{2,1,0:T(8,128)(2,1)S(1)}, bf16[4,160,128]{2,1,0:T(8,128)(2,1)S(1)}, u32[]{:S(2)}, u32[]{:S(2)}) collective-permute-start(bf16[4,160,128]{2,1,0:T(8,128)(2,1)S(1)} %get-tuple-element.49.refs_10_), channel_id=1, source_target_pairs={{17,26},{19,28},{21,30},{18,25},{20,27},{22,29}} | collective-permute-start | bytes 491528 | tf_op jit(solution)/shard_map/ppermute | solution.py:391
  76.4 6.3 %collective-permute-start.16 = (bf16[4,160,128]{2,1,0:T(8,128)(2,1)S(1)}, bf16[4,160,128]{2,1,0:T(8,128)(2,1)S(1)}, u32[]{:S(2)}, u32[]{:S(2)}) collective-permute-start(bf16[4,160,128]{2,1,0:T(8,128)(2,1)S(1)} %collective-permute-done.15.refs_0_), channel_id=1, source_target_pairs={{24,25},{25,24},{26,27},{27,26},{28,29},{29,28},{30,31},{31,30}} | collective-permute-start | bytes 491528 | tf_op jit(solution)/shard_map/ppermute | solution.py:388
